TPU v7x, 32 devices: a whole 2x2x4 slice. The times are simulated.
32 devices in a mesh: alpha: 16 (over z, y, x), beta: 2 (over core).
Axes of the slice: x: 2, y: 2, z: 4, core: 2. Of those that a mesh axis runs over, the one named last changes fastest.
Arguments:
- coeffs: bfloat16 [1024, 512], P('alpha', 'beta'), may hold values from -6 to 6
- integrals: bfloat16 [484, 484], replicated, may hold values from -0.0234375 to 0.0234375
- send_block: int32 [16, 128], P('alpha'), may hold values from 0 to 16, as said below
- alpha_slot: int32 [256, 132], P('alpha'), may hold values from 0 to 63, as said below
- alpha_pair: int32 [256, 132], P('alpha'), may hold values from 0 to 483, as said below
- alpha_parity: int32 [256, 132], P('alpha'), may hold values from 0 to 1
- beta_pair: int32 [32, 132], P('beta'), may hold values from 0 to 483, as said below
- beta_target: int32 [32, 132], P('beta'), may hold values from 0 to 31
- beta_parity: int32 [32, 132], P('beta'), may hold values from 0 to 1
Outputs:
- sigma: float32 [1024, 512], P('alpha', 'beta')
Inputs may be any that keep to these rules, and one draw needn't show every extreme that they name: `send_block`: in each batch the filled slots from one sender to one receiver come first; at most 4 are filled, 4 is reached from every sender to some receiver in every batch, and some slots stay empty in every batch. `alpha_slot`: every entry names a slot that holds a block. `alpha_pair`: the pairs of one row are distinct. `beta_pair`: the pairs of one row are distinct.
All inputs are finite; a program needn't handle non-finite values.
Results may differ from a plain program's by a relative error of at most 0.0003.
Values may be sent and summed in bfloat16 or wider, within the bound.
No kernel may reach another device: no remote copies, remote signals or barrier semaphores. Data moves between devices by JAX's collectives and lax.ppermute only.
A program may use at most 64 MiB of HBM per device.

v0:
```python
import jax
import jax.numpy as jnp
from jax import lax
from jax.experimental import pallas as pl
from jax.experimental.pallas import tpu as pltpu
from jax.sharding import PartitionSpec as P

BATCHES = 2
CAP = 4
BF = jnp.bfloat16
F32 = jnp.float32
LANES = 128
WIDE = 256


def row_of(length):
    return lax.broadcasted_iota(jnp.int32, (1, length), 1)


def column_of(length):
    return lax.broadcasted_iota(jnp.int32, (length, 1), 0)


def over(x, n):
    if n & (n - 1) == 0:
        return lax.shift_right_logical(x, jnp.int32(n.bit_length() - 1))
    return lax.div(x, jnp.int32(n))


def modulo(x, n):
    if n & (n - 1) == 0:
        return x & (n - 1)
    return lax.rem(x, jnp.int32(n))


def one(condition):
    return jnp.where(condition, 1.0, 0.0).astype(BF)


def dot(a, b):
    return jnp.dot(a, b, preferred_element_type=F32)


def dot_nt(a, b):
    return lax.dot_general(a, b, (((1,), (1,)), ((), ())), preferred_element_type=F32)


def split(x):
    high = x.astype(BF)
    return high, (x - high.astype(F32)).astype(BF)


def collect_kernel(*refs):
    count = (len(refs) - 5) // 2
    coeffs_ref, send_ref = refs[:2]
    others, chunks_ref, copies = refs[2 : 2 + count], refs[2 + count], refs[3 + count : -2]
    list_ref, sems = refs[-2:]
    chunks, total, columns = chunks_ref.shape
    rows, slots = coeffs_ref.shape[0], send_ref.shape[1]
    pairs = [(send_ref, list_ref)]
    pairs += [(coeffs_ref, chunks_ref.at[k, pl.ds(0, rows)]) for k in range(chunks)]
    pairs += list(zip(others, copies))
    moves = [
        pltpu.make_async_copy(source, target, sems.at[i]) for i, (source, target) in enumerate(pairs)
    ]
    for move in moves:
        move.start()
    moves[0].wait()
    values = list_ref[...].astype(F32)
    value = jnp.zeros((total - rows, columns), F32)
    for i, first in enumerate(range(0, slots, columns)):
        row = values[:, first : first + columns]
        if row.shape[1] < columns:
            row = jnp.concatenate([row, jnp.zeros((1, columns - row.shape[1]), F32)], axis=1)
        value = value + jnp.where(column_of(total - rows) == i, row, 0.0)
    for k in range(chunks):
        chunks_ref[k, rows:total, :] = value.astype(BF)
    for move in moves[1:]:
        move.wait()


def forward_kernel(strings, width, inner, rows, slots, gathered_ref, out_ref):
    outer, _, columns = gathered_ref.shape
    wide = strings * columns
    group = strings * width
    per = BATCHES * CAP
    blocks = rows // strings
    n = row_of(wide)
    spread = one(column_of(columns) == over(n, group) * width + modulo(n, width))
    gathered = jnp.concatenate([gathered_ref[k, :rows, :] for k in range(outer)], axis=0)
    keep = modulo(column_of(outer * rows), strings) == modulo(over(n, width), strings)
    spaced = jnp.where(keep, dot(gathered, spread), 0.0).astype(BF)
    r = column_of(inner * per)
    receiver = over(lax.axis_index("alpha"), inner) * inner + over(r, per)
    wanted = over(modulo(r, per), CAP) * (slots // BATCHES) + receiver * CAP + modulo(r, CAP)
    wanted = wanted == row_of(slots)
    picks = []
    for k in range(outer):
        tail = gathered_ref[k, rows:, :].astype(F32)
        listed = [tail[i : i + 1] for i in range((slots + columns - 1) // columns)]
        listed = (listed[0] if len(listed) == 1 else jnp.concatenate(listed, axis=1))[:, :slots]
        chosen = jnp.sum(jnp.where(wanted, listed, 0.0), axis=1, keepdims=True).astype(jnp.int32)
        chosen = jnp.where(chosen < blocks, chosen + k * blocks, -1)
        picks.append(jnp.where(over(row_of(outer * rows), strings) == chosen, 1.0, 0.0))
    for j in range(inner):
        pick = jnp.concatenate([part[j * per : (j + 1) * per] for part in picks], axis=0)
        out_ref[j] = dot(pick.astype(BF), spaced).astype(BF)


def tables_kernel(
    beta_blocks,
    outer,
    inner,
    slot_ref,
    pair_ref,
    parity_ref,
    bpair_ref,
    btarget_ref,
    bparity_ref,
    integrals_ref,
    _,
    out_ref,
    t_ref,
    w_ref,
    hot_ref,
):
    orbitals = integrals_ref.shape[0]
    blocks, excitations = slot_ref.shape
    beta_local, beta_excitations = bpair_ref.shape
    pairs = blocks // BATCHES
    slots = hot_ref.shape[0] // pairs
    bpair = bpair_ref[...].astype(F32).T.astype(jnp.int32)
    bfactor = (1 - 2 * bparity_ref[...]).astype(F32)
    btarget = btarget_ref[...] - lax.axis_index("beta") * beta_local
    btarget = jnp.where(btarget < 0, btarget + beta_blocks, btarget)
    for v in range(beta_local):
        left = jnp.where(column_of(beta_blocks) == btarget[v : v + 1], bfactor[v : v + 1], 0.0)
        right = one(row_of(orbitals) == bpair[:, v : v + 1])
        t_ref[v * beta_blocks : (v + 1) * beta_blocks, :] = dot(left.astype(BF), right).astype(BF)
    high, low = split(dot(t_ref[...], integrals_ref[...]))
    w_ref[0] = high
    w_ref[1] = low
    pair = pair_ref[...].astype(F32).T.astype(jnp.int32)
    factor = (1 - 2 * parity_ref[...]).astype(F32)
    slot = slot_ref[...]
    sender = over(slot, CAP)
    place = modulo(sender, inner) * outer + over(sender, inner)
    place = place * (BATCHES * CAP) + modulo(slot, CAP)
    for t in range(pairs):
        total = None
        for h in range(BATCHES):
            g = h * pairs + t
            row = place[g : g + 1] + h * CAP
            left = jnp.where(column_of(slots) == row, factor[g : g + 1], 0.0).astype(BF)
            part = dot(left, one(row_of(orbitals) == pair[:, g : g + 1]))
            total = part if total is None else total + part
        hot_ref[t * slots : (t + 1) * slots, :] = total.astype(BF)
    step = max(1, WIDE // slots)
    for start in range(0, pairs, step):
        hot = hot_ref[start * slots : (start + step) * slots, :]
        high, low = split(dot_nt(w_ref[0], hot) + dot_nt(w_ref[1], hot))
        for i in range(step):
            rows = slice((start + i) * beta_blocks, (start + i + 1) * beta_blocks)
            lanes = slice(i * slots, (i + 1) * slots)
            for v in range(beta_local):
                source = slice(v * beta_blocks, (v + 1) * beta_blocks)
                first = v * 2 * slots
                out_ref[rows, first : first + slots] = high[source, lanes]
                out_ref[rows, first + slots : first + 2 * slots] = low[source, lanes]


def sigma_kernel(strings, width, table_ref, received_ref, *refs):
    outs, (right_ref, sum_ref, place_ref) = refs[:-3], refs[-3:]
    slots, wide = received_ref.shape
    group = strings * width
    both = BATCHES * group
    pairs = outs[0].shape[0] // strings // BATCHES
    blocks = table_ref.shape[0] // pairs
    batch = modulo(over(column_of(slots), CAP), BATCHES)
    low = one((batch == 0) & (row_of(both) < group))
    high = one((batch == 1) & (row_of(both) >= group))
    for tile in range(wide // both):
        x = received_ref[:, tile * both : (tile + 1) * both]
        turned = jnp.concatenate([x[:, group:], x[:, :group]], axis=1)
        for v, (a, b) in ((2 * tile, (x, turned)), (2 * tile + 1, (turned, x))):
            value = a * low + b * high
            right_ref[2 * v * slots : (2 * v + 1) * slots, :] = value
            right_ref[(2 * v + 1) * slots : (2 * v + 2) * slots, :] = value
    product = dot(table_ref[...], right_ref[...])
    both_parts = jnp.concatenate(split(product), axis=1)
    per_tile = LANES // width
    columns = BATCHES * strings * LANES
    n = row_of(columns)
    expand = one(
        modulo(column_of(2 * both), both) == over(n, LANES) * width + modulo(n, width)
    )
    spread = dot(both_parts, expand)
    keep = modulo(column_of(pairs * blocks), per_tile) == modulo(over(n, width), per_tile)
    spread = jnp.where(keep, spread, 0.0)
    tiles = blocks // per_tile
    summed = jnp.sum(spread.reshape(pairs * tiles, per_tile, columns), axis=1)
    for hs in range(BATCHES * strings):
        sum_ref[hs] = summed[:, hs * LANES : (hs + 1) * LANES]
    per_out = tiles // len(outs)
    for q in range(tiles):
        for h in range(BATCHES):
            for s in range(strings):
                place_ref[q, pl.ds(h * pairs * strings + s, pairs, stride=strings), :] = sum_ref[
                    h * strings + s, pl.ds(q, pairs, stride=tiles), :
                ]
        at = q % per_out * LANES
        outs[q // per_out][:, at : at + LANES] = place_ref[q]


def on_device(
    coeffs,
    integrals,
    send_block,
    alpha_slot,
    alpha_pair,
    alpha_parity,
    beta_pair,
    beta_target,
    beta_parity,
):
    local_rows, local_columns = coeffs.shape
    local_blocks = alpha_slot.shape[0]
    strings = local_rows // local_blocks
    pairs = local_blocks // BATCHES
    beta_local = beta_pair.shape[0]
    width = local_columns // beta_local
    cores = lax.axis_size("beta")
    senders = lax.axis_size("alpha")
    beta_blocks = cores * beta_local
    orbitals = integrals.shape[0]
    slots = send_block.shape[1]
    wide = strings * local_columns

    outer = 1 << (senders.bit_length() - 1) // 2
    inner = senders // outer
    per = slots // senders

    extra = -(-slots // local_columns // 16) * 16
    others = (
        alpha_slot,
        alpha_pair,
        alpha_parity,
        beta_pair,
        beta_target,
        beta_parity,
        integrals,
    )
    chunks = (outer, local_rows + extra, local_columns)
    chunks, *tables = pl.pallas_call(
        collect_kernel,
        in_specs=[pl.BlockSpec(memory_space=pltpu.HBM)] * (2 + len(others)),
        out_shape=[jax.ShapeDtypeStruct(chunks, BF)]
        + [jax.ShapeDtypeStruct(x.shape, x.dtype) for x in others],
        scratch_shapes=[
            pltpu.VMEM(send_block.shape, jnp.int32),
            pltpu.SemaphoreType.DMA((1 + outer + len(others),)),
        ],
        compiler_params=pltpu.CompilerParams(vmem_limit_bytes=40 * 2**20),
        name="collect",
    )(*(pltpu.with_memory_space_constraint(x, pltpu.HBM) for x in (coeffs, send_block, *others)))
    along = [[k * inner + i for k in range(outer)] for i in range(inner)]
    across = [[k * inner + i for i in range(inner)] for k in range(outer)]
    gathered = lax.all_to_all(chunks, "alpha", 0, 0, axis_index_groups=along, tiled=True)
    outgoing = pl.pallas_call(
        lambda *refs: forward_kernel(strings, width, inner, local_rows, slots, *refs),
        out_shape=jax.ShapeDtypeStruct((inner, outer * per, wide), BF),
        compiler_params=pltpu.CompilerParams(vmem_limit_bytes=40 * 2**20),
        name="forward",
    )(gathered)
    received = lax.all_to_all(outgoing, "alpha", 0, 0, axis_index_groups=across, tiled=True)
    received = received.reshape(slots, wide)
    flops = 2 * beta_local * beta_blocks * orbitals * (orbitals + 2 * pairs * slots)
    table = pl.pallas_call(
        lambda *refs: tables_kernel(beta_blocks, outer, inner, *refs),
        in_specs=[pl.BlockSpec(memory_space=pltpu.VMEM)] * len(tables)
        + [pl.BlockSpec(memory_space=pl.ANY)],
        out_shape=jax.ShapeDtypeStruct((pairs * beta_blocks, 2 * beta_local * slots), BF),
        scratch_shapes=[
            pltpu.VMEM((beta_local * beta_blocks, orbitals), BF),
            pltpu.VMEM((2, beta_local * beta_blocks, orbitals), BF),
            pltpu.VMEM((pairs * slots, orbitals), BF),
        ],
        compiler_params=pltpu.CompilerParams(vmem_limit_bytes=40 * 2**20),
        cost_estimate=pl.CostEstimate(flops=flops, bytes_accessed=8 * 2**20, transcendentals=0),
        name="tables",
    )(*tables, outgoing)
    part = jax.ShapeDtypeStruct((local_rows, local_columns), F32)
    both = BATCHES * strings * width
    tiles = beta_blocks * width // LANES
    parts = pl.pallas_call(
        lambda *refs: sigma_kernel(strings, width, *refs),
        out_shape=[part] * cores,
        scratch_shapes=[
            pltpu.VMEM((2 * beta_local * slots, both), BF),
            pltpu.VMEM((BATCHES * strings, pairs * tiles, LANES), F32),
            pltpu.VMEM((tiles, local_rows, LANES), F32),
        ],
        compiler_params=pltpu.CompilerParams(vmem_limit_bytes=40 * 2**20),
        name="sigma",
    )(table, received)
    result = parts[0]
    for step in range(1, cores):
        route = [(core, (core + step) % cores) for core in range(cores)]
        result = result + lax.ppermute(parts[step], "beta", route)
    return result


def solution(mesh):
    in_specs = (
        P("alpha", "beta"),
        P(),
        P("alpha", None),
        P("alpha", None),
        P("alpha", None),
        P("alpha", None),
        P("beta", None),
        P("beta", None),
        P("beta", None),
    )
    out_specs = P("alpha", "beta")
    return jax.shard_map(
        on_device, mesh=mesh, in_specs=in_specs, out_specs=out_specs, check_vma=False
    )
```

profile of v0, /device:TPU:0, one launch (start us, length us, event | category | flops | bytes accessed | tf_op | source)
XLA Modules:
  0.0 28.0 jit_solution(5519942467778702240)
XLA Ops:
  0.0 1.3 %collect.1 = (bf16[4,80,256]{2,1,0:T(8,128)(2,1)S(1)}, s32[16,132]{1,0:T(8,128)S(1)}, s32[16,132]{1,0:T(8,128)S(1)}, s32[16,132]{1,0:T(8,128)S(1)}, s32[16,132]{...) custom-call(bf16[64,256]{1,0:T(8,128)(2,1)} %refs_0_.1, ...), custom_call_target="tpu_custom_call" | custom-call | tf_op jit(solution)/shard_map/collect/pallas_call | solution.py:254
  1.3 13.1 %all_to_all.10.refs_0_ = bf16[4,80,256]{2,1,0:T(8,128)(2,1)S(1)} all-to-all(bf16[4,80,256]{2,1,0:T(8,128)(2,1)S(1)} %get-tuple-element.22), channel_id=1, replica_groups={{0,8,16,24},{2,10,18,26},{4,12,20,28},{6,14,22,30},{1,9,17,25},{3,11,19..., dimensions={0} | all-to-all | bytes 327680 | tf_op jit(solution)/shard_map/all_to_all | solution.py:268
  14.4 1.4 %forward.1.refs_7_ = bf16[4,32,1024]{2,1,0:T(8,128)(2,1)} custom-call(bf16[4,80,256]{2,1,0:T(8,128)(2,1)S(1)} %all_to_all.10.refs_0_), custom_call_target="tpu_custom_call" | custom-call | tf_op jit(solution)/shard_map/forward/pallas_call | solution.py:269
  15.8 3.7 %all-to-all-start.1 = ((bf16[4,32,1024]{2,1,0:T(8,128)(2,1)}), bf16[4,32,1024]{2,1,0:T(8,128)(2,1)S(1)}, u32[]{:S(2)}, u32[]{:S(2)}) async-start(bf16[4,32,1024]{2,1,0:T(8,128)(2,1)} %forward.1.refs_7_), calls=%async_computation.1 | async-start | bytes 524288 | tf_op jit(solution)/shard_map/all_to_all | solution.py:275
  19.5 3.0 %tables.1.refs_0_ = bf16[256,4096]{1,0:T(8,128)(2,1)S(1)} custom-call(s32[16,132]{1,0:T(8,128)S(1)} %get-tuple-element.15.refs_0_, s32[16,132]{1,0:T(8,128)S(1)} %get-tuple-element.16.refs_1_, s32[16,132]{1,0:T(8,128)S(1)} %get-tuple-element.17.refs_2_, s32[16,132]{1,0:T(8,128)S(1)} %get-tuple-element.18.refs_3_, s32[16,132]{1,0:T(8,128)S(1)} %get-tuple-element.19.refs_4_, ...), custom_call_target="tpu_custom_call" | custom-call | flops 1254899712 | bytes 8388608 | tf_op jit(solution)/shard_map/tables/pallas_call | solution.py:278
  22.5 2.3 %all-to-all-done.1 = bf16[4,32,1024]{2,1,0:T(8,128)(2,1)S(1)} async-done(((bf16[4,32,1024]{2,1,0:T(8,128)(2,1)}), bf16[4,32,1024]{2,1,0:T(8,128)(2,1)S(1)}, u32[]{:S(2)}, u32[]{:S(2)}) %all-to-all-start.1) | async-done | bytes 262176 | tf_op jit(solution)/shard_map/all_to_all | solution.py:275
  24.9 1.2 %sigma.1 = (f32[64,256]{1,0:T(8,128)S(1)}, f32[64,256]{1,0:T(8,128)S(1)}) custom-call(bf16[256,4096]{1,0:T(8,128)(2,1)S(1)} %tables.1.refs_0_, bf16[128,1024]{1,0:T(8,128)(2,1)S(1)} %bitcast.1), custom_call_target="tpu_custom_call" | custom-call | tf_op jit(solution)/shard_map/sigma/pallas_call | solution.py:295
  26.1 0.1 collective-permute-start
  26.2 1.2 %collective-permute-done = f32[64,256]{1,0:T(8,128)S(1)} collective-permute-done((f32[64,256]{1,0:T(8,128)S(1)}, f32[64,256]{1,0:T(8,128)S(1)}, u32[]{:S(2)}, u32[]{:S(2)}) %collective-permute-start) | collective-permute-done | bytes 65568 | tf_op jit(solution)/shard_map/ppermute | solution.py:309
  27.4 0.6 %add.3 = f32[64,256]{1,0:T(8,128)} add(f32[64,256]{1,0:T(8,128)S(1)} %get-tuple-element.23, f32[64,256]{1,0:T(8,128)S(1)} %collective-permute-done) | non-fusion elementwise | flops 16384 | bytes 196608 | tf_op jit(solution)/shard_map/add | solution.py:309
Async XLA Ops:
  15.8 9.1 %all-to-all-start.1 = ((bf16[4,32,1024]{2,1,0:T(8,128)(2,1)}), bf16[4,32,1024]{2,1,0:T(8,128)(2,1)S(1)}, u32[]{:S(2)}, u32[]{:S(2)}) async-start(bf16[4,32,1024]{2,1,0:T(8,128)(2,1)} %forward.1.refs_7_), calls=%async_computation.1 | async-start | bytes 524288 | tf_op jit(solution)/shard_map/all_to_all | solution.py:275
  26.1 1.3 %collective-permute-start = (f32[64,256]{1,0:T(8,128)S(1)}, f32[64,256]{1,0:T(8,128)S(1)}, u32[]{:S(2)}, u32[]{:S(2)}) collective-permute-start(f32[64,256]{1,0:T(8,128)S(1)} %get-tuple-element.24), channel_id=1, source_target_pairs={{0,1},{1,0},{2,3},{3,2},{4,5},{5,4},{6,7},{7,6},{8,9},{9,8},{10,11... | collective-permute-start | bytes 196616 | tf_op jit(solution)/shard_map/ppermute | solution.py:309
where the time goes:
time: 28.3 us; the launch traced here: 28 us
  blocking collectives  13.1 us (46%)
  Pallas kernels  6.93 us (24%)
  starting transfers between devices  3.79 us (13%)
  waiting for transfers between devices  3.58 us (13%)
  other arithmetic  0.64 us (2%)
    all_to_all x1, blocking collectives, on_device(): lax.all_to_all(chunks, 'alpha', 0, 0, axis_index_groups=along, tiled=True)  13.1 us
    all_to_all x1, starting transfers between devices, on_device(): lax.all_to_all(outgoing, 'alpha', 0, 0, axis_index_groups=across, tiled=T...  3.72 us
    pallas_call x1, Pallas kernels, on_device(): pl.pallas_call(lambda *refs: tables_kernel(beta_blocks, outer, inner, *re...  3.03 us
    all_to_all x1, waiting for transfers between devices, on_device(): lax.all_to_all(outgoing, 'alpha', 0, 0, axis_index_groups=across, tiled=T...  2.34 us
    pallas_call x1, Pallas kernels, on_device(): pl.pallas_call(lambda *refs: forward_kernel(strings, width, inner, local_...  1.41 us
    pallas_call x1, Pallas kernels, on_device(): pl.pallas_call(collect_kernel, in_specs=[pl.BlockSpec(memory_space=pltpu....  1.3 us
    ppermute x1, waiting for transfers between devices, on_device(): result = result + lax.ppermute(parts[step], 'beta', route)  1.24 us
    pallas_call x1, Pallas kernels, on_device(): pl.pallas_call(lambda *refs: sigma_kernel(strings, width, *refs), out_sha...  1.2 us
  transfers between devices with their start and end apart: 2, of which 2 were waited for; matrix products, arithmetic and copies ran while one was open for 0% of the time, Pallas kernels for 11%

commit v1 on v0

--- a/solution.py
+++ b/solution.py
@@ -50,18 +50,12 @@
     return high, (x - high.astype(F32)).astype(BF)
 
 
-def collect_kernel(*refs):
-    count = (len(refs) - 5) // 2
-    coeffs_ref, send_ref = refs[:2]
-    others, chunks_ref, copies = refs[2 : 2 + count], refs[2 + count], refs[3 + count : -2]
-    list_ref, sems = refs[-2:]
-    chunks, total, columns = chunks_ref.shape
+def pack_kernel(coeffs_ref, send_ref, out_ref, list_ref, sems):
     rows, slots = coeffs_ref.shape[0], send_ref.shape[1]
-    pairs = [(send_ref, list_ref)]
-    pairs += [(coeffs_ref, chunks_ref.at[k, pl.ds(0, rows)]) for k in range(chunks)]
-    pairs += list(zip(others, copies))
+    total, columns = out_ref.shape
     moves = [
-        pltpu.make_async_copy(source, target, sems.at[i]) for i, (source, target) in enumerate(pairs)
+        pltpu.make_async_copy(send_ref, list_ref, sems.at[0]),
+        pltpu.make_async_copy(coeffs_ref, out_ref.at[pl.ds(0, rows)], sems.at[1]),
     ]
     for move in moves:
         move.start()
@@ -73,30 +67,41 @@
         if row.shape[1] < columns:
             row = jnp.concatenate([row, jnp.zeros((1, columns - row.shape[1]), F32)], axis=1)
         value = value + jnp.where(column_of(total - rows) == i, row, 0.0)
-    for k in range(chunks):
-        chunks_ref[k, rows:total, :] = value.astype(BF)
-    for move in moves[1:]:
+    out_ref[rows:total, :] = value.astype(BF)
+    moves[1].wait()
+
+
+def fetch_kernel(*refs):
+    count = (len(refs) - 2) // 2
+    moves = [
+        pltpu.make_async_copy(refs[i], refs[count + 1 + i], refs[-1].at[i]) for i in range(count)
+    ]
+    for move in moves:
+        move.start()
+    for move in moves:
         move.wait()
 
 
-def forward_kernel(strings, width, inner, rows, slots, gathered_ref, out_ref):
-    outer, _, columns = gathered_ref.shape
+def forward_kernel(strings, width, rows, slots, outer, *refs):
+    gathered_refs, out_refs = refs[:outer], refs[outer:]
+    inner = len(out_refs)
+    columns = gathered_refs[0].shape[1]
     wide = strings * columns
     group = strings * width
     per = BATCHES * CAP
     blocks = rows // strings
     n = row_of(wide)
     spread = one(column_of(columns) == over(n, group) * width + modulo(n, width))
-    gathered = jnp.concatenate([gathered_ref[k, :rows, :] for k in range(outer)], axis=0)
+    gathered = jnp.concatenate([ref[:rows, :] for ref in gathered_refs], axis=0)
     keep = modulo(column_of(outer * rows), strings) == modulo(over(n, width), strings)
     spaced = jnp.where(keep, dot(gathered, spread), 0.0).astype(BF)
     r = column_of(inner * per)
-    receiver = over(lax.axis_index("alpha"), inner) * inner + over(r, per)
+    receiver = over(r, per) ^ lax.axis_index("alpha")
     wanted = over(modulo(r, per), CAP) * (slots // BATCHES) + receiver * CAP + modulo(r, CAP)
     wanted = wanted == row_of(slots)
     picks = []
     for k in range(outer):
-        tail = gathered_ref[k, rows:, :].astype(F32)
+        tail = gathered_refs[k][rows:, :].astype(F32)
         listed = [tail[i : i + 1] for i in range((slots + columns - 1) // columns)]
         listed = (listed[0] if len(listed) == 1 else jnp.concatenate(listed, axis=1))[:, :slots]
         chosen = jnp.sum(jnp.where(wanted, listed, 0.0), axis=1, keepdims=True).astype(jnp.int32)
@@ -104,7 +109,7 @@
         picks.append(jnp.where(over(row_of(outer * rows), strings) == chosen, 1.0, 0.0))
     for j in range(inner):
         pick = jnp.concatenate([part[j * per : (j + 1) * per] for part in picks], axis=0)
-        out_ref[j] = dot(pick.astype(BF), spaced).astype(BF)
+        out_refs[j][...] = dot(pick.astype(BF), spaced).astype(BF)
 
 
 def tables_kernel(
@@ -143,8 +148,8 @@
     pair = pair_ref[...].astype(F32).T.astype(jnp.int32)
     factor = (1 - 2 * parity_ref[...]).astype(F32)
     slot = slot_ref[...]
-    sender = over(slot, CAP)
-    place = modulo(sender, inner) * outer + over(sender, inner)
+    partner = over(slot, CAP) ^ lax.axis_index("alpha")
+    place = modulo(partner, inner) * outer + over(partner, inner)
     place = place * (BATCHES * CAP) + modulo(slot, CAP)
     for t in range(pairs):
         total = None
@@ -169,9 +174,10 @@
                 out_ref[rows, first + slots : first + 2 * slots] = low[source, lanes]
 
 
-def sigma_kernel(strings, width, table_ref, received_ref, *refs):
-    outs, (right_ref, sum_ref, place_ref) = refs[:-3], refs[-3:]
-    slots, wide = received_ref.shape
+def sigma_kernel(strings, width, inner, table_ref, *refs):
+    received_refs, outs, (right_ref, sum_ref, place_ref) = refs[:inner], refs[inner:-3], refs[-3:]
+    received = jnp.concatenate([ref[...] for ref in received_refs], axis=0)
+    slots, wide = received.shape
     group = strings * width
     both = BATCHES * group
     pairs = outs[0].shape[0] // strings // BATCHES
@@ -180,7 +186,7 @@
     low = one((batch == 0) & (row_of(both) < group))
     high = one((batch == 1) & (row_of(both) >= group))
     for tile in range(wide // both):
-        x = received_ref[:, tile * both : (tile + 1) * both]
+        x = received[:, tile * both : (tile + 1) * both]
         turned = jnp.concatenate([x[:, group:], x[:, :group]], axis=1)
         for v, (a, b) in ((2 * tile, (x, turned)), (2 * tile + 1, (turned, x))):
             value = a * low + b * high
@@ -250,30 +256,40 @@
         beta_parity,
         integrals,
     )
-    chunks = (outer, local_rows + extra, local_columns)
-    chunks, *tables = pl.pallas_call(
-        collect_kernel,
-        in_specs=[pl.BlockSpec(memory_space=pltpu.HBM)] * (2 + len(others)),
-        out_shape=[jax.ShapeDtypeStruct(chunks, BF)]
-        + [jax.ShapeDtypeStruct(x.shape, x.dtype) for x in others],
+    def exchange(x, k):
+        return lax.ppermute(x, "alpha", [(d, d ^ k) for d in range(senders)]) if k else x
+
+    def pinned(*arrays):
+        return [pltpu.with_memory_space_constraint(x, pltpu.HBM) for x in arrays]
+
+    packed = pl.pallas_call(
+        pack_kernel,
+        in_specs=[pl.BlockSpec(memory_space=pltpu.HBM)] * 2,
+        out_shape=jax.ShapeDtypeStruct((local_rows + extra, local_columns), BF),
         scratch_shapes=[
             pltpu.VMEM(send_block.shape, jnp.int32),
-            pltpu.SemaphoreType.DMA((1 + outer + len(others),)),
+            pltpu.SemaphoreType.DMA((2,)),
         ],
         compiler_params=pltpu.CompilerParams(vmem_limit_bytes=40 * 2**20),
-        name="collect",
-    )(*(pltpu.with_memory_space_constraint(x, pltpu.HBM) for x in (coeffs, send_block, *others)))
-    along = [[k * inner + i for k in range(outer)] for i in range(inner)]
-    across = [[k * inner + i for i in range(inner)] for k in range(outer)]
-    gathered = lax.all_to_all(chunks, "alpha", 0, 0, axis_index_groups=along, tiled=True)
+        name="pack",
+    )(*pinned(coeffs, send_block))
+    gathered = [exchange(packed, k * inner) for k in range(outer)]
+    tables = pl.pallas_call(
+        fetch_kernel,
+        in_specs=[pl.BlockSpec(memory_space=pltpu.HBM)] * len(others)
+        + [pl.BlockSpec(memory_space=pl.ANY)],
+        out_shape=[jax.ShapeDtypeStruct(x.shape, x.dtype) for x in others],
+        scratch_shapes=[pltpu.SemaphoreType.DMA((len(others),))],
+        compiler_params=pltpu.CompilerParams(vmem_limit_bytes=40 * 2**20),
+        name="fetch",
+    )(*pinned(*others), packed)
     outgoing = pl.pallas_call(
-        lambda *refs: forward_kernel(strings, width, inner, local_rows, slots, *refs),
-        out_shape=jax.ShapeDtypeStruct((inner, outer * per, wide), BF),
+        lambda *refs: forward_kernel(strings, width, local_rows, slots, outer, *refs),
+        out_shape=[jax.ShapeDtypeStruct((outer * per, wide), BF)] * inner,
         compiler_params=pltpu.CompilerParams(vmem_limit_bytes=40 * 2**20),
         name="forward",
-    )(gathered)
-    received = lax.all_to_all(outgoing, "alpha", 0, 0, axis_index_groups=across, tiled=True)
-    received = received.reshape(slots, wide)
+    )(*gathered)
+    received = [exchange(x, j) for j, x in enumerate(outgoing)]
     flops = 2 * beta_local * beta_blocks * orbitals * (orbitals + 2 * pairs * slots)
     table = pl.pallas_call(
         lambda *refs: tables_kernel(beta_blocks, outer, inner, *refs),
@@ -288,12 +304,12 @@
         compiler_params=pltpu.CompilerParams(vmem_limit_bytes=40 * 2**20),
         cost_estimate=pl.CostEstimate(flops=flops, bytes_accessed=8 * 2**20, transcendentals=0),
         name="tables",
-    )(*tables, outgoing)
+    )(*tables, outgoing[0])
     part = jax.ShapeDtypeStruct((local_rows, local_columns), F32)
     both = BATCHES * strings * width
     tiles = beta_blocks * width // LANES
     parts = pl.pallas_call(
-        lambda *refs: sigma_kernel(strings, width, *refs),
+        lambda *refs: sigma_kernel(strings, width, inner, *refs),
         out_shape=[part] * cores,
         scratch_shapes=[
             pltpu.VMEM((2 * beta_local * slots, both), BF),
@@ -302,7 +318,7 @@
         ],
         compiler_params=pltpu.CompilerParams(vmem_limit_bytes=40 * 2**20),
         name="sigma",
-    )(table, received)
+    )(table, *received)
     result = parts[0]
     for step in range(1, cores):
         route = [(core, (core + step) % cores) for core in range(cores)]

time: 28.3 us -> 23.2 us (0.82)
  blocking collectives: 13.1 us -> 0 us
  starting transfers between devices: 3.79 us -> 9.37 us
  waiting for transfers between devices: 3.58 us -> 5.92 us
    all_to_all x1 -> x0, blocking collectives: 13.1 us -> none  [on_device(): lax.all_to_all(chunks, 'alpha', 0, 0, axis_index_groups=along, tiled=True)]
    ppermute x0 -> x6, starting transfers between devices: none -> 9.3 us  [exchange(): lax.ppermute(x, 'alpha', [(d, d ^ k) for d in range(senders)])]
    ppermute x0 -> x6, waiting for transfers between devices: none -> 4.68 us  [exchange(): lax.ppermute(x, 'alpha', [(d, d ^ k) for d in range(senders)])]
    all_to_all x1 -> x0, starting transfers between devices: 3.72 us -> none  [on_device(): lax.all_to_all(outgoing, 'alpha', 0, 0, axis_index_groups=across, tiled=T...]
    all_to_all x1 -> x0, waiting for transfers between devices: 2.34 us -> none  [on_device(): lax.all_to_all(outgoing, 'alpha', 0, 0, axis_index_groups=across, tiled=T...]
    pallas_call x3 -> x4, Pallas kernels: 3.91 us -> 3.9 us  [the longest x1 1.21 us: on_device(): pl.pallas_call(lambda *refs: sigma_kernel(strings, width, inner, *refs),...]
  transfers between devices with their start and end apart: 2 -> 7, of which waited for: 2 -> 4; matrix products, arithmetic and copies ran while one was open for 0% -> 0% of each run, Pallas kernels for 11% -> 19%
where the time goes in v1:
time: 23.2 us; the launch traced here: 22.9 us
  starting transfers between devices  9.37 us (40%)
  Pallas kernels  6.95 us (30%)
  waiting for transfers between devices  5.92 us (26%)
  other arithmetic  0.64 us (3%)
    ppermute x6, starting transfers between devices, exchange(): lax.ppermute(x, 'alpha', [(d, d ^ k) for d in range(senders)])  9.3 us
    ppermute x6, waiting for transfers between devices, exchange(): lax.ppermute(x, 'alpha', [(d, d ^ k) for d in range(senders)])  4.68 us
    pallas_call x1, Pallas kernels, on_device(): pl.pallas_call(lambda *refs: tables_kernel(beta_blocks, outer, inner, *re...  3.04 us
    ppermute x1, waiting for transfers between devices, on_device(): result = result + lax.ppermute(parts[step], 'beta', route)  1.24 us
    pallas_call x1, Pallas kernels, on_device(): pl.pallas_call(lambda *refs: sigma_kernel(strings, width, inner, *refs),...  1.21 us
    pallas_call x1, Pallas kernels, on_device(): pl.pallas_call(fetch_kernel, in_specs=[pl.BlockSpec(memory_space=pltpu.HB...  1.2 us
    pallas_call x1, Pallas kernels, on_device(): pl.pallas_call(pack_kernel, in_specs=[pl.BlockSpec(memory_space=pltpu.HBM...  0.79 us
    pallas_call x1, Pallas kernels, on_device(): pl.pallas_call(lambda *refs: forward_kernel(strings, width, local_rows, s...  0.71 us
  transfers between devices with their start and end apart: 7, of which 4 were waited for; matrix products, arithmetic and copies ran while one was open for 0% of the time, Pallas kernels for 19%

profile of v1, /device:TPU:0, one launch (start us, length us, event | category | flops | bytes accessed | tf_op | source)
XLA Modules:
  0.0 22.9 jit_solution(7918787415257851429)
XLA Ops:
  0.0 0.8 %pack.1.refs_7_.refs_0_ = bf16[80,256]{1,0:T(8,128)(2,1)S(1)} custom-call(bf16[64,256]{1,0:T(8,128)(2,1)} %coeffs_ref.1, s32[1,128]{1,0:T(1,128)} %send_ref.1), custom_call_target="tpu_custom_call" | custom-call | tf_op jit(solution)/shard_map/pack/pallas_call | solution.py:265
  0.8 5.1 %collective-permute-start.2 = (bf16[80,256]{1,0:T(8,128)(2,1)S(1)}, bf16[80,256]{1,0:T(8,128)(2,1)S(1)}, u32[]{:S(2)}, u32[]{:S(2)}) collective-permute-start(bf16[80,256]{1,0:T(8,128)(2,1)S(1)} %pack.1.refs_7_.refs_0_), channel_id=1, source_target_pairs={{0,24},{2,26},{4,28},{6,30},{8,16},{10,18},{12,20},{14,22},{16,8},... | collective-permute-start | bytes 122888 | tf_op jit(solution)/shard_map/ppermute | solution.py:260
  5.9 0.0 collective-permute-start.1
  5.9 0.6 %collective-permute-start = (bf16[80,256]{1,0:T(8,128)(2,1)S(1)}, bf16[80,256]{1,0:T(8,128)(2,1)S(1)}, u32[]{:S(2)}, u32[]{:S(2)}) collective-permute-start(bf16[80,256]{1,0:T(8,128)(2,1)S(1)} %pack.1.refs_7_.refs_0_), channel_id=1, source_target_pairs={{0,8},{2,10},{4,12},{6,14},{8,0},{10,2},{12,4},{14,6},{16,24},{18,... | collective-permute-start | bytes 122888 | tf_op jit(solution)/shard_map/ppermute | solution.py:260
  6.6 1.2 %fetch.1 = (s32[16,132]{1,0:T(8,128)S(1)}, s32[16,132]{1,0:T(8,128)S(1)}, s32[16,132]{1,0:T(8,128)S(1)}, s32[16,132]{1,0:T(8,128)S(1)}, s32[16,132]{1,0:T(8,128)...) custom-call(s32[16,132]{1,0:T(8,128)} %refs_0_.1, s32[16,132]{1,0:T(8,128)} %refs_1_.1, s32[16,132]{1,0:T(8,128)} %refs_2_.1, ...), custom_call_target="tpu_custom_call" | custom-call | tf_op jit(solution)/shard_map/fetch/pallas_call | solution.py:277
  7.8 0.2 collective-permute-done.2.refs_3_
  7.9 2.9 %collective-permute-done.1.refs_2_ = bf16[80,256]{1,0:T(8,128)(2,1)S(1)} collective-permute-done((bf16[80,256]{1,0:T(8,128)(2,1)S(1)}, bf16[80,256]{1,0:T(8,128)(2,1)S(1)}, u32[]{:S(2)}, u32[]{:S(2)}) %collective-permute-start.1) | collective-permute-done | bytes 40992 | tf_op jit(solution)/shard_map/ppermute | solution.py:260
  10.8 0.0 collective-permute-done.refs_1_
  10.8 0.7 %forward.1 = (bf16[32,1024]{1,0:T(8,128)(2,1)S(1)}, bf16[32,1024]{1,0:T(8,128)(2,1)S(1)}, bf16[32,1024]{1,0:T(8,128)(2,1)S(1)}, bf16[32,1024]{1,0:T(8,128)(2,1)S(1)}) custom-call(bf16[80,256]{1,0:T(8,128)(2,1)S(1)} %pack.1.refs_7_.refs_0_, bf16[80,256]{1,0:T(8,128)(2,1)S(1)} %collective-permute-done.refs_1_, ...), custom_call_target="tpu_custom_call" | custom-call | tf_op jit(solution)/shard_map/forward/pallas_call | solution.py:286
  11.5 1.5 %collective-permute-start.3 = (bf16[32,1024]{1,0:T(8,128)(2,1)S(1)}, bf16[32,1024]{1,0:T(8,128)(2,1)S(1)}, u32[]{:S(2)}, u32[]{:S(2)}) collective-permute-start(bf16[32,1024]{1,0:T(8,128)(2,1)S(1)} %get-tuple-element.26), channel_id=1, source_target_pairs={{0,2},{2,0},{4,6},{6,4},{8,10},{10,8},{12,14},{14,12},{16,18},{18,... | collective-permute-start | bytes 196616 | tf_op jit(solution)/shard_map/ppermute | solution.py:260
  13.1 1.5 %collective-permute-start.4 = (bf16[32,1024]{1,0:T(8,128)(2,1)S(1)}, bf16[32,1024]{1,0:T(8,128)(2,1)S(1)}, u32[]{:S(2)}, u32[]{:S(2)}) collective-permute-start(bf16[32,1024]{1,0:T(8,128)(2,1)S(1)} %get-tuple-element.27), channel_id=1, source_target_pairs={{0,4},{2,6},{4,0},{6,2},{8,12},{10,14},{12,8},{14,10},{16,20},{18,... | collective-permute-start | bytes 196616 | tf_op jit(solution)/shard_map/ppermute | solution.py:260
  14.6 0.5 %collective-permute-start.5 = (bf16[32,1024]{1,0:T(8,128)(2,1)S(1)}, bf16[32,1024]{1,0:T(8,128)(2,1)S(1)}, u32[]{:S(2)}, u32[]{:S(2)}) collective-permute-start(bf16[32,1024]{1,0:T(8,128)(2,1)S(1)} %get-tuple-element.28), channel_id=1, source_target_pairs={{0,6},{2,4},{4,2},{6,0},{8,14},{10,12},{12,10},{14,8},{16,22},{18,... | collective-permute-start | bytes 196616 | tf_op jit(solution)/shard_map/ppermute | solution.py:260
  15.1 3.0 %tables.1.refs_0_ = bf16[256,4096]{1,0:T(8,128)(2,1)S(1)} custom-call(s32[16,132]{1,0:T(8,128)S(1)} %get-tuple-element.18.refs_0_, s32[16,132]{1,0:T(8,128)S(1)} %get-tuple-element.19.refs_1_, s32[16,132]{1,0:T(8,128)S(1)} %get-tuple-element.20.refs_2_, s32[16,132]{1,0:T(8,128)S(1)} %get-tuple-element.21.refs_3_, s32[16,132]{1,0:T(8,128)S(1)} %get-tuple-element.22.refs_4_, ...), custom_call_target="tpu_custom_call" | custom-call | flops 1254899712 | bytes 8388608 | tf_op jit(solution)/shard_map/tables/pallas_call | solution.py:294
  18.1 0.0 collective-permute-done.3.refs_2_
  18.1 0.0 collective-permute-done.4.refs_3_
  18.1 1.6 %collective-permute-done.5.refs_4_ = bf16[32,1024]{1,0:T(8,128)(2,1)S(1)} collective-permute-done((bf16[32,1024]{1,0:T(8,128)(2,1)S(1)}, bf16[32,1024]{1,0:T(8,128)(2,1)S(1)}, u32[]{:S(2)}, u32[]{:S(2)}) %collective-permute-start.5) | collective-permute-done | bytes 65568 | tf_op jit(solution)/shard_map/ppermute | solution.py:260
  19.8 1.2 %sigma.1 = (f32[64,256]{1,0:T(8,128)S(1)}, f32[64,256]{1,0:T(8,128)S(1)}) custom-call(bf16[256,4096]{1,0:T(8,128)(2,1)S(1)} %tables.1.refs_0_, bf16[32,1024]{1,0:T(8,128)(2,1)S(1)} %get-tuple-element.25.refs_7_.refs_1_, bf16[32,1024]{1,0:T(8,128)(2,1)S(1)} %collective-permute-done.3.refs_2_, bf16[32,1024]{1,0:T(8,128)(2,1)S(1)} %collective-permute-done.4.refs_3_, ...), custom_call_target="tpu_custom_call" | custom-call | tf_op jit(solution)/shard_map/sigma/pallas_call | solution.py:311
  21.0 0.1 collective-permute-start.6
  21.1 1.2 %collective-permute-done.6 = f32[64,256]{1,0:T(8,128)S(1)} collective-permute-done((f32[64,256]{1,0:T(8,128)S(1)}, f32[64,256]{1,0:T(8,128)S(1)}, u32[]{:S(2)}, u32[]{:S(2)}) %collective-permute-start.6) | collective-permute-done | bytes 65568 | tf_op jit(solution)/shard_map/ppermute | solution.py:325
  22.3 0.6 %add.3 = f32[64,256]{1,0:T(8,128)} add(f32[64,256]{1,0:T(8,128)S(1)} %get-tuple-element.29, f32[64,256]{1,0:T(8,128)S(1)} %collective-permute-done.6) | non-fusion elementwise | flops 16384 | bytes 196608 | tf_op jit(solution)/shard_map/add | solution.py:325
Async XLA Ops:
  0.8 7.1 %collective-permute-start.2 = (bf16[80,256]{1,0:T(8,128)(2,1)S(1)}, bf16[80,256]{1,0:T(8,128)(2,1)S(1)}, u32[]{:S(2)}, u32[]{:S(2)}) collective-permute-start(bf16[80,256]{1,0:T(8,128)(2,1)S(1)} %pack.1.refs_7_.refs_0_), channel_id=1, source_target_pairs={{0,24},{2,26},{4,28},{6,30},{8,16},{10,18},{12,20},{14,22},{16,8},... | collective-permute-start | bytes 122888 | tf_op jit(solution)/shard_map/ppermute | solution.py:260
  5.9 4.9 %collective-permute-start.1 = (bf16[80,256]{1,0:T(8,128)(2,1)S(1)}, bf16[80,256]{1,0:T(8,128)(2,1)S(1)}, u32[]{:S(2)}, u32[]{:S(2)}) collective-permute-start(bf16[80,256]{1,0:T(8,128)(2,1)S(1)} %pack.1.refs_7_.refs_0_), channel_id=1, source_target_pairs={{0,16},{2,18},{4,20},{6,22},{8,24},{10,26},{12,28},{14,30},{16,0},... | collective-permute-start | bytes 122888 | tf_op jit(solution)/shard_map/ppermute | solution.py:260
  5.9 4.9 %collective-permute-start = (bf16[80,256]{1,0:T(8,128)(2,1)S(1)}, bf16[80,256]{1,0:T(8,128)(2,1)S(1)}, u32[]{:S(2)}, u32[]{:S(2)}) collective-permute-start(bf16[80,256]{1,0:T(8,128)(2,1)S(1)} %pack.1.refs_7_.refs_0_), channel_id=1, source_target_pairs={{0,8},{2,10},{4,12},{6,14},{8,0},{10,2},{12,4},{14,6},{16,24},{18,... | collective-permute-start | bytes 122888 | tf_op jit(solution)/shard_map/ppermute | solution.py:260
  11.5 6.6 %collective-permute-start.3 = (bf16[32,1024]{1,0:T(8,128)(2,1)S(1)}, bf16[32,1024]{1,0:T(8,128)(2,1)S(1)}, u32[]{:S(2)}, u32[]{:S(2)}) collective-permute-start(bf16[32,1024]{1,0:T(8,128)(2,1)S(1)} %get-tuple-element.26), channel_id=1, source_target_pairs={{0,2},{2,0},{4,6},{6,4},{8,10},{10,8},{12,14},{14,12},{16,18},{18,... | collective-permute-start | bytes 196616 | tf_op jit(solution)/shard_map/ppermute | solution.py:260
  13.1 5.1 %collective-permute-start.4 = (bf16[32,1024]{1,0:T(8,128)(2,1)S(1)}, bf16[32,1024]{1,0:T(8,128)(2,1)S(1)}, u32[]{:S(2)}, u32[]{:S(2)}) collective-permute-start(bf16[32,1024]{1,0:T(8,128)(2,1)S(1)} %get-tuple-element.27), channel_id=1, source_target_pairs={{0,4},{2,6},{4,0},{6,2},{8,12},{10,14},{12,8},{14,10},{16,20},{18,... | collective-permute-start | bytes 196616 | tf_op jit(solution)/shard_map/ppermute | solution.py:260
  14.6 5.2 %collective-permute-start.5 = (bf16[32,1024]{1,0:T(8,128)(2,1)S(1)}, bf16[32,1024]{1,0:T(8,128)(2,1)S(1)}, u32[]{:S(2)}, u32[]{:S(2)}) collective-permute-start(bf16[32,1024]{1,0:T(8,128)(2,1)S(1)} %get-tuple-element.28), channel_id=1, source_target_pairs={{0,6},{2,4},{4,2},{6,0},{8,14},{10,12},{12,10},{14,8},{16,22},{18,... | collective-permute-start | bytes 196616 | tf_op jit(solution)/shard_map/ppermute | solution.py:260
  21.0 1.3 %collective-permute-start.6 = (f32[64,256]{1,0:T(8,128)S(1)}, f32[64,256]{1,0:T(8,128)S(1)}, u32[]{:S(2)}, u32[]{:S(2)}) collective-permute-start(f32[64,256]{1,0:T(8,128)S(1)} %get-tuple-element.30), channel_id=1, source_target_pairs={{0,1},{1,0},{2,3},{3,2},{4,5},{5,4},{6,7},{7,6},{8,9},{9,8},{10,11... | collective-permute-start | bytes 196616 | tf_op jit(solution)/shard_map/ppermute | solution.py:325

commit v2 on v1

--- a/solution.py
+++ b/solution.py
@@ -71,13 +71,19 @@
     moves[1].wait()
 
 
-def fetch_kernel(*refs):
-    count = (len(refs) - 2) // 2
+def fetch_kernel(width, *refs):
+    count = (len(refs) - 3) // 2
+    expand_ref, sems = refs[-2:]
     moves = [
-        pltpu.make_async_copy(refs[i], refs[count + 1 + i], refs[-1].at[i]) for i in range(count)
+        pltpu.make_async_copy(refs[i], refs[count + 1 + i], sems.at[i]) for i in range(count)
     ]
     for move in moves:
         move.start()
+    rows, columns = expand_ref.shape
+    n = row_of(columns)
+    expand_ref[...] = one(
+        modulo(column_of(rows), rows // 2) == over(n, LANES) * width + modulo(n, width)
+    )
     for move in moves:
         move.wait()
 
@@ -165,23 +171,24 @@
         hot = hot_ref[start * slots : (start + step) * slots, :]
         high, low = split(dot_nt(w_ref[0], hot) + dot_nt(w_ref[1], hot))
         for i in range(step):
-            rows = slice((start + i) * beta_blocks, (start + i + 1) * beta_blocks)
             lanes = slice(i * slots, (i + 1) * slots)
             for v in range(beta_local):
-                source = slice(v * beta_blocks, (v + 1) * beta_blocks)
                 first = v * 2 * slots
-                out_ref[rows, first : first + slots] = high[source, lanes]
-                out_ref[rows, first + slots : first + 2 * slots] = low[source, lanes]
-
-
-def sigma_kernel(strings, width, inner, table_ref, *refs):
-    received_refs, outs, (right_ref, sum_ref, place_ref) = refs[:inner], refs[inner:-3], refs[-3:]
+                for part in range(beta_blocks // beta_local):
+                    row = (part * pairs + start + i) * beta_local
+                    rows = slice(row, row + beta_local)
+                    row = v * beta_blocks + part * beta_local
+                    source = slice(row, row + beta_local)
+                    out_ref[rows, first : first + slots] = high[source, lanes]
+                    out_ref[rows, first + slots : first + 2 * slots] = low[source, lanes]
+
+
+def right_kernel(strings, width, inner, *refs):
+    received_refs, (table_ref, expand_ref, right_ref), rest = refs[:inner], refs[inner : inner + 3], refs[inner + 3 :]
     received = jnp.concatenate([ref[...] for ref in received_refs], axis=0)
     slots, wide = received.shape
     group = strings * width
     both = BATCHES * group
-    pairs = outs[0].shape[0] // strings // BATCHES
-    blocks = table_ref.shape[0] // pairs
     batch = modulo(over(column_of(slots), CAP), BATCHES)
     low = one((batch == 0) & (row_of(both) < group))
     high = one((batch == 1) & (row_of(both) >= group))
@@ -192,30 +199,32 @@
             value = a * low + b * high
             right_ref[2 * v * slots : (2 * v + 1) * slots, :] = value
             right_ref[(2 * v + 1) * slots : (2 * v + 2) * slots, :] = value
-    product = dot(table_ref[...], right_ref[...])
+    sigma_kernel(strings, width, 1, right_ref, table_ref, expand_ref, *rest)
+
+
+def sigma_kernel(strings, width, part, right_ref, table_ref, expand_ref, out_ref, sum_ref, place_ref):
+    local_rows, columns = out_ref.shape
+    pairs = local_rows // strings // BATCHES
+    blocks = columns // width
+    rows = pairs * blocks
+    product = dot(table_ref[part * rows : (part + 1) * rows, :], right_ref[...])
     both_parts = jnp.concatenate(split(product), axis=1)
     per_tile = LANES // width
-    columns = BATCHES * strings * LANES
-    n = row_of(columns)
-    expand = one(
-        modulo(column_of(2 * both), both) == over(n, LANES) * width + modulo(n, width)
-    )
-    spread = dot(both_parts, expand)
-    keep = modulo(column_of(pairs * blocks), per_tile) == modulo(over(n, width), per_tile)
+    spread = dot(both_parts, expand_ref[...])
+    wide = spread.shape[1]
+    keep = modulo(column_of(rows), per_tile) == modulo(over(row_of(wide), width), per_tile)
     spread = jnp.where(keep, spread, 0.0)
     tiles = blocks // per_tile
-    summed = jnp.sum(spread.reshape(pairs * tiles, per_tile, columns), axis=1)
+    summed = jnp.sum(spread.reshape(pairs * tiles, per_tile, wide), axis=1)
     for hs in range(BATCHES * strings):
         sum_ref[hs] = summed[:, hs * LANES : (hs + 1) * LANES]
-    per_out = tiles // len(outs)
     for q in range(tiles):
         for h in range(BATCHES):
             for s in range(strings):
                 place_ref[q, pl.ds(h * pairs * strings + s, pairs, stride=strings), :] = sum_ref[
                     h * strings + s, pl.ds(q, pairs, stride=tiles), :
                 ]
-        at = q % per_out * LANES
-        outs[q // per_out][:, at : at + LANES] = place_ref[q]
+        out_ref[:, q * LANES : (q + 1) * LANES] = place_ref[q]
 
 
 def on_device(
@@ -274,11 +283,13 @@
         name="pack",
     )(*pinned(coeffs, send_block))
     gathered = [exchange(packed, k * inner) for k in range(outer)]
-    tables = pl.pallas_call(
-        fetch_kernel,
+    both = BATCHES * strings * width
+    *tables, expand = pl.pallas_call(
+        lambda *refs: fetch_kernel(width, *refs),
         in_specs=[pl.BlockSpec(memory_space=pltpu.HBM)] * len(others)
         + [pl.BlockSpec(memory_space=pl.ANY)],
-        out_shape=[jax.ShapeDtypeStruct(x.shape, x.dtype) for x in others],
+        out_shape=[jax.ShapeDtypeStruct(x.shape, x.dtype) for x in others]
+        + [jax.ShapeDtypeStruct((2 * both, BATCHES * strings * LANES), BF)],
         scratch_shapes=[pltpu.SemaphoreType.DMA((len(others),))],
         compiler_params=pltpu.CompilerParams(vmem_limit_bytes=40 * 2**20),
         name="fetch",
@@ -306,23 +317,43 @@
         name="tables",
     )(*tables, outgoing[0])
     part = jax.ShapeDtypeStruct((local_rows, local_columns), F32)
-    both = BATCHES * strings * width
-    tiles = beta_blocks * width // LANES
-    parts = pl.pallas_call(
-        lambda *refs: sigma_kernel(strings, width, inner, *refs),
-        out_shape=[part] * cores,
+    tiles = local_columns // LANES
+    call = dict(
         scratch_shapes=[
-            pltpu.VMEM((2 * beta_local * slots, both), BF),
             pltpu.VMEM((BATCHES * strings, pairs * tiles, LANES), F32),
             pltpu.VMEM((tiles, local_rows, LANES), F32),
         ],
         compiler_params=pltpu.CompilerParams(vmem_limit_bytes=40 * 2**20),
-        name="sigma",
-    )(table, *received)
-    result = parts[0]
-    for step in range(1, cores):
-        route = [(core, (core + step) % cores) for core in range(cores)]
-        result = result + lax.ppermute(parts[step], "beta", route)
+        cost_estimate=pl.CostEstimate(
+            flops=4 * pairs * slots * beta_local * beta_local * both,
+            bytes_accessed=3 * 2**20,
+            transcendentals=0,
+        ),
+    )
+    right, theirs = pl.pallas_call(
+        lambda *refs: right_kernel(strings, width, inner, *refs),
+        out_shape=[jax.ShapeDtypeStruct((2 * beta_local * slots, both), BF), part],
+        name="theirs",
+        **call,
+    )(*received, table, expand)
+
+    def route(step):
+        return [(core, (core + step) % cores) for core in range(cores)]
+
+    arrived = [lax.ppermute(theirs, "beta", route(1))]
+    for step in range(2, cores):
+        other = pl.pallas_call(
+            lambda *refs, step=step: sigma_kernel(strings, width, step, *refs),
+            out_shape=part,
+            name="theirs%d" % step,
+            **call,
+        )(right, table, expand)
+        arrived.append(lax.ppermute(other, "beta", route(step)))
+    result = pl.pallas_call(
+        lambda *refs: sigma_kernel(strings, width, 0, *refs), out_shape=part, name="mine", **call
+    )(right, table, expand)
+    for value in arrived:
+        result = result + value
     return result
 
 

time: 23.2 us -> 22.8 us (0.983)
  waiting for transfers between devices: 5.92 us -> 5.26 us
  Pallas kernels: 6.95 us -> 7.22 us
    ppermute x1, waiting for transfers between devices: 1.24 us -> 0.53 us  [on_device(): arrived = [lax.ppermute(theirs, 'beta', route(1))]]
    pallas_call x2 -> x3, Pallas kernels: 2.4 us -> 2.74 us  [the longest x1 1.2 us: on_device(): pl.pallas_call(lambda *refs: fetch_kernel(width, *refs), in_specs=[pl.Blo...]
  transfers between devices with their start and end apart: 7 -> 7, of which waited for: 4 -> 4; matrix products, arithmetic and copies ran while one was open for 0% -> 0% of each run, Pallas kernels for 19% -> 22%
where the time goes in v2:
time: 22.8 us; the launch traced here: 22.5 us
  starting transfers between devices  9.36 us (41%)
  Pallas kernels  7.22 us (32%)
  waiting for transfers between devices  5.26 us (23%)
  other arithmetic  0.64 us (3%)
    ppermute x6, starting transfers between devices, exchange(): lax.ppermute(x, 'alpha', [(d, d ^ k) for d in range(senders)])  9.3 us
    ppermute x6, waiting for transfers between devices, exchange(): lax.ppermute(x, 'alpha', [(d, d ^ k) for d in range(senders)])  4.74 us
    pallas_call x1, Pallas kernels, on_device(): pl.pallas_call(lambda *refs: tables_kernel(beta_blocks, outer, inner, *re...  2.98 us
    pallas_call x1, Pallas kernels, on_device(): pl.pallas_call(lambda *refs: fetch_kernel(width, *refs), in_specs=[pl.Blo...  1.2 us
    pallas_call x1, Pallas kernels, on_device(): pl.pallas_call(lambda *refs: right_kernel(strings, width, inner, *refs),...  0.82 us
    pallas_call x1, Pallas kernels, on_device(): pl.pallas_call(pack_kernel, in_specs=[pl.BlockSpec(memory_space=pltpu.HBM...  0.79 us
    pallas_call x1, Pallas kernels, on_device(): pl.pallas_call(lambda *refs: sigma_kernel(strings, width, 0, *refs), out_...  0.72 us
    pallas_call x1, Pallas kernels, on_device(): pl.pallas_call(lambda *refs: forward_kernel(strings, width, local_rows, s...  0.71 us
  transfers between devices with their start and end apart: 7, of which 4 were waited for; matrix products, arithmetic and copies ran while one was open for 0% of the time, Pallas kernels for 22%

profile of v2, /device:TPU:0, one launch (start us, length us, event | category | flops | bytes accessed | tf_op | source)
XLA Modules:
  0.0 22.5 jit_solution(5547343963979038323)
XLA Ops:
  0.0 0.8 %pack.1.refs_0_.refs_7_ = bf16[80,256]{1,0:T(8,128)(2,1)S(1)} custom-call(bf16[64,256]{1,0:T(8,128)(2,1)} %coeffs_ref.1, s32[1,128]{1,0:T(1,128)} %send_ref.1), custom_call_target="tpu_custom_call" | custom-call | tf_op jit(solution)/shard_map/pack/pallas_call | solution.py:274
  0.8 5.1 %collective-permute-start.2 = (bf16[80,256]{1,0:T(8,128)(2,1)S(1)}, bf16[80,256]{1,0:T(8,128)(2,1)S(1)}, u32[]{:S(2)}, u32[]{:S(2)}) collective-permute-start(bf16[80,256]{1,0:T(8,128)(2,1)S(1)} %pack.1.refs_0_.refs_7_), channel_id=1, source_target_pairs={{0,24},{2,26},{4,28},{6,30},{8,16},{10,18},{12,20},{14,22},{16,8},... | collective-permute-start | bytes 122888 | tf_op jit(solution)/shard_map/ppermute | solution.py:269
  5.9 0.0 collective-permute-start.1
  5.9 0.6 %collective-permute-start = (bf16[80,256]{1,0:T(8,128)(2,1)S(1)}, bf16[80,256]{1,0:T(8,128)(2,1)S(1)}, u32[]{:S(2)}, u32[]{:S(2)}) collective-permute-start(bf16[80,256]{1,0:T(8,128)(2,1)S(1)} %pack.1.refs_0_.refs_7_), channel_id=1, source_target_pairs={{0,8},{2,10},{4,12},{6,14},{8,0},{10,2},{12,4},{14,6},{16,24},{18,... | collective-permute-start | bytes 122888 | tf_op jit(solution)/shard_map/ppermute | solution.py:269
  6.6 1.2 %fetch.1 = (s32[16,132]{1,0:T(8,128)S(1)}, s32[16,132]{1,0:T(8,128)S(1)}, s32[16,132]{1,0:T(8,128)S(1)}, s32[16,132]{1,0:T(8,128)S(1)}, s32[16,132]{1,0:T(8,128)...) custom-call(s32[16,132]{1,0:T(8,128)} %refs_0_.1, s32[16,132]{1,0:T(8,128)} %refs_1_.1, ...), custom_call_target="tpu_custom_call" | custom-call | tf_op jit(solution)/shard_map/fetch/pallas_call | solution.py:287
  7.8 0.2 collective-permute-done.2.refs_3_
  7.9 2.9 %collective-permute-done.1.refs_2_ = bf16[80,256]{1,0:T(8,128)(2,1)S(1)} collective-permute-done((bf16[80,256]{1,0:T(8,128)(2,1)S(1)}, bf16[80,256]{1,0:T(8,128)(2,1)S(1)}, u32[]{:S(2)}, u32[]{:S(2)}) %collective-permute-start.1) | collective-permute-done | bytes 40992 | tf_op jit(solution)/shard_map/ppermute | solution.py:269
  10.8 0.0 collective-permute-done.refs_1_
  10.8 0.7 %forward.1 = (bf16[32,1024]{1,0:T(8,128)(2,1)S(1)}, bf16[32,1024]{1,0:T(8,128)(2,1)S(1)}, bf16[32,1024]{1,0:T(8,128)(2,1)S(1)}, bf16[32,1024]{1,0:T(8,128)(2,1)S(1)}) custom-call(bf16[80,256]{1,0:T(8,128)(2,1)S(1)} %pack.1.refs_0_.refs_7_, bf16[80,256]{1,0:T(8,128)(2,1)S(1)} %collective-permute-done.refs_1_, ...), custom_call_target="tpu_custom_call" | custom-call | tf_op jit(solution)/shard_map/forward/pallas_call | solution.py:297
  11.5 1.5 %collective-permute-start.3 = (bf16[32,1024]{1,0:T(8,128)(2,1)S(1)}, bf16[32,1024]{1,0:T(8,128)(2,1)S(1)}, u32[]{:S(2)}, u32[]{:S(2)}) collective-permute-start(bf16[32,1024]{1,0:T(8,128)(2,1)S(1)} %get-tuple-element.20), channel_id=1, source_target_pairs={{0,2},{2,0},{4,6},{6,4},{8,10},{10,8},{12,14},{14,12},{16,18},{18,... | collective-permute-start | bytes 196616 | tf_op jit(solution)/shard_map/ppermute | solution.py:269
  13.1 1.5 %collective-permute-start.4 = (bf16[32,1024]{1,0:T(8,128)(2,1)S(1)}, bf16[32,1024]{1,0:T(8,128)(2,1)S(1)}, u32[]{:S(2)}, u32[]{:S(2)}) collective-permute-start(bf16[32,1024]{1,0:T(8,128)(2,1)S(1)} %get-tuple-element.21), channel_id=1, source_target_pairs={{0,4},{2,6},{4,0},{6,2},{8,12},{10,14},{12,8},{14,10},{16,20},{18,... | collective-permute-start | bytes 196616 | tf_op jit(solution)/shard_map/ppermute | solution.py:269
  14.6 0.5 %collective-permute-start.5 = (bf16[32,1024]{1,0:T(8,128)(2,1)S(1)}, bf16[32,1024]{1,0:T(8,128)(2,1)S(1)}, u32[]{:S(2)}, u32[]{:S(2)}) collective-permute-start(bf16[32,1024]{1,0:T(8,128)(2,1)S(1)} %get-tuple-element.22), channel_id=1, source_target_pairs={{0,6},{2,4},{4,2},{6,0},{8,14},{10,12},{12,10},{14,8},{16,22},{18,... | collective-permute-start | bytes 196616 | tf_op jit(solution)/shard_map/ppermute | solution.py:269
  15.1 3.0 %tables.1.refs_4_.refs_1_ = bf16[256,4096]{1,0:T(8,128)(2,1)S(1)} custom-call(s32[16,132]{1,0:T(8,128)S(1)} %get-tuple-element.23.refs_0_, s32[16,132]{1,0:T(8,128)S(1)} %get-tuple-element.24.refs_1_, s32[16,132]{1,0:T(8,128)S(1)} %get-tuple-element.25.refs_2_, s32[16,132]{1,0:T(8,128)S(1)} %get-tuple-element.26.refs_3_, ...), custom_call_target="tpu_custom_call" | custom-call | flops 1254899712 | bytes 8388608 | tf_op jit(solution)/shard_map/tables/pallas_call | solution.py:305
  18.1 0.0 collective-permute-done.3.refs_1_
  18.1 0.0 collective-permute-done.4.refs_2_
  18.1 1.7 %collective-permute-done.5.refs_3_ = bf16[32,1024]{1,0:T(8,128)(2,1)S(1)} collective-permute-done((bf16[32,1024]{1,0:T(8,128)(2,1)S(1)}, bf16[32,1024]{1,0:T(8,128)(2,1)S(1)}, u32[]{:S(2)}, u32[]{:S(2)}) %collective-permute-start.5) | collective-permute-done | bytes 65568 | tf_op jit(solution)/shard_map/ppermute | solution.py:269
  19.8 0.8 %theirs.1 = (bf16[4096,128]{1,0:T(8,128)(2,1)S(1)}, f32[64,256]{1,0:T(8,128)S(1)}) custom-call(bf16[32,1024]{1,0:T(8,128)(2,1)S(1)} %get-tuple-element.19.refs_7_.refs_0_, bf16[32,1024]{1,0:T(8,128)(2,1)S(1)} %collective-permute-done.3.refs_1_, bf16[32,1024]{1,0:T(8,128)(2,1)S(1)} %collective-permute-done.4.refs_2_, ...), custom_call_target="tpu_custom_call" | custom-call | flops 134217728 | bytes 3145728 | tf_op jit(solution)/shard_map/theirs/pallas_call | solution.py:333
  20.6 0.1 collective-permute-start.6
  20.7 0.7 %mine.1 = f32[64,256]{1,0:T(8,128)S(1)} custom-call(bf16[4096,128]{1,0:T(8,128)(2,1)S(1)} %get-tuple-element.31.refs_0_, bf16[256,4096]{1,0:T(8,128)(2,1)S(1)} %tables.1.refs_4_.refs_1_, bf16[256,1024]{1,0:T(8,128)(2,1)S(1)} %get-tuple-element.30.refs_5_.refs_2_), custom_call_target="tpu_custom_call" | custom-call | flops 134217728 | bytes 3145728 | tf_op jit(solution)/shard_map/mine/pallas_call | solution.py:352
  21.4 0.5 %collective-permute-done.6 = f32[64,256]{1,0:T(8,128)S(1)} collective-permute-done((f32[64,256]{1,0:T(8,128)S(1)}, f32[64,256]{1,0:T(8,128)S(1)}, u32[]{:S(2)}, u32[]{:S(2)}) %collective-permute-start.6) | collective-permute-done | bytes 65568 | tf_op jit(solution)/shard_map/ppermute | solution.py:343
  21.9 0.6 %add.3 = f32[64,256]{1,0:T(8,128)} add(f32[64,256]{1,0:T(8,128)S(1)} %mine.1, f32[64,256]{1,0:T(8,128)S(1)} %collective-permute-done.6) | non-fusion elementwise | flops 16384 | bytes 196608 | tf_op jit(solution)/shard_map/add | solution.py:356
Async XLA Ops:
  0.8 7.1 %collective-permute-start.2 = (bf16[80,256]{1,0:T(8,128)(2,1)S(1)}, bf16[80,256]{1,0:T(8,128)(2,1)S(1)}, u32[]{:S(2)}, u32[]{:S(2)}) collective-permute-start(bf16[80,256]{1,0:T(8,128)(2,1)S(1)} %pack.1.refs_0_.refs_7_), channel_id=1, source_target_pairs={{0,24},{2,26},{4,28},{6,30},{8,16},{10,18},{12,20},{14,22},{16,8},... | collective-permute-start | bytes 122888 | tf_op jit(solution)/shard_map/ppermute | solution.py:269
  5.9 4.9 %collective-permute-start.1 = (bf16[80,256]{1,0:T(8,128)(2,1)S(1)}, bf16[80,256]{1,0:T(8,128)(2,1)S(1)}, u32[]{:S(2)}, u32[]{:S(2)}) collective-permute-start(bf16[80,256]{1,0:T(8,128)(2,1)S(1)} %pack.1.refs_0_.refs_7_), channel_id=1, source_target_pairs={{0,16},{2,18},{4,20},{6,22},{8,24},{10,26},{12,28},{14,30},{16,0},... | collective-permute-start | bytes 122888 | tf_op jit(solution)/shard_map/ppermute | solution.py:269
  5.9 4.9 %collective-permute-start = (bf16[80,256]{1,0:T(8,128)(2,1)S(1)}, bf16[80,256]{1,0:T(8,128)(2,1)S(1)}, u32[]{:S(2)}, u32[]{:S(2)}) collective-permute-start(bf16[80,256]{1,0:T(8,128)(2,1)S(1)} %pack.1.refs_0_.refs_7_), channel_id=1, source_target_pairs={{0,8},{2,10},{4,12},{6,14},{8,0},{10,2},{12,4},{14,6},{16,24},{18,... | collective-permute-start | bytes 122888 | tf_op jit(solution)/shard_map/ppermute | solution.py:269
  11.5 6.5 %collective-permute-start.3 = (bf16[32,1024]{1,0:T(8,128)(2,1)S(1)}, bf16[32,1024]{1,0:T(8,128)(2,1)S(1)}, u32[]{:S(2)}, u32[]{:S(2)}) collective-permute-start(bf16[32,1024]{1,0:T(8,128)(2,1)S(1)} %get-tuple-element.20), channel_id=1, source_target_pairs={{0,2},{2,0},{4,6},{6,4},{8,10},{10,8},{12,14},{14,12},{16,18},{18,... | collective-permute-start | bytes 196616 | tf_op jit(solution)/shard_map/ppermute | solution.py:269
  13.1 5.0 %collective-permute-start.4 = (bf16[32,1024]{1,0:T(8,128)(2,1)S(1)}, bf16[32,1024]{1,0:T(8,128)(2,1)S(1)}, u32[]{:S(2)}, u32[]{:S(2)}) collective-permute-start(bf16[32,1024]{1,0:T(8,128)(2,1)S(1)} %get-tuple-element.21), channel_id=1, source_target_pairs={{0,4},{2,6},{4,0},{6,2},{8,12},{10,14},{12,8},{14,10},{16,20},{18,... | collective-permute-start | bytes 196616 | tf_op jit(solution)/shard_map/ppermute | solution.py:269
  14.6 5.2 %collective-permute-start.5 = (bf16[32,1024]{1,0:T(8,128)(2,1)S(1)}, bf16[32,1024]{1,0:T(8,128)(2,1)S(1)}, u32[]{:S(2)}, u32[]{:S(2)}) collective-permute-start(bf16[32,1024]{1,0:T(8,128)(2,1)S(1)} %get-tuple-element.22), channel_id=1, source_target_pairs={{0,6},{2,4},{4,2},{6,0},{8,14},{10,12},{12,10},{14,8},{16,22},{18,... | collective-permute-start | bytes 196616 | tf_op jit(solution)/shard_map/ppermute | solution.py:269
  20.6 1.3 %collective-permute-start.6 = (f32[64,256]{1,0:T(8,128)S(1)}, f32[64,256]{1,0:T(8,128)S(1)}, u32[]{:S(2)}, u32[]{:S(2)}) collective-permute-start(f32[64,256]{1,0:T(8,128)S(1)} %get-tuple-element.32), channel_id=1, source_target_pairs={{0,1},{1,0},{2,3},{3,2},{4,5},{5,4},{6,7},{7,6},{8,9},{9,8},{10,11... | collective-permute-start | bytes 196616 | tf_op jit(solution)/shard_map/ppermute | solution.py:343

commit v3 on v2

--- a/solution.py
+++ b/solution.py
@@ -88,8 +88,8 @@
         move.wait()
 
 
-def forward_kernel(strings, width, rows, slots, outer, *refs):
-    gathered_refs, out_refs = refs[:outer], refs[outer:]
+def forward_kernel(strings, width, rows, slots, outer, turn, *refs):
+    gathered_refs, out_refs = [refs[turn.index(k)] for k in range(outer)], refs[outer:]
     inner = len(out_refs)
     columns = gathered_refs[0].shape[1]
     wide = strings * columns
@@ -282,7 +282,10 @@
         compiler_params=pltpu.CompilerParams(vmem_limit_bytes=40 * 2**20),
         name="pack",
     )(*pinned(coeffs, send_block))
-    gathered = [exchange(packed, k * inner) for k in range(outer)]
+    bits = outer.bit_length() - 1
+    starts = sorted(range(outer), key=lambda k: int(format(k, "0%db" % bits)[::-1], 2))
+    turn = starts[:1] + starts[:0:-1]
+    gathered = [exchange(packed, k * inner) for k in turn]
     both = BATCHES * strings * width
     *tables, expand = pl.pallas_call(
         lambda *refs: fetch_kernel(width, *refs),
@@ -295,7 +298,7 @@
         name="fetch",
     )(*pinned(*others), packed)
     outgoing = pl.pallas_call(
-        lambda *refs: forward_kernel(strings, width, local_rows, slots, outer, *refs),
+        lambda *refs: forward_kernel(strings, width, local_rows, slots, outer, turn, *refs),
         out_shape=[jax.ShapeDtypeStruct((outer * per, wide), BF)] * inner,
         compiler_params=pltpu.CompilerParams(vmem_limit_bytes=40 * 2**20),
         name="forward",

time: 22.8 us -> 24.2 us (1.061)
  waiting for transfers between devices: 5.26 us -> 6.79 us
    ppermute x6, waiting for transfers between devices: 4.74 us -> 6.27 us  [exchange(): lax.ppermute(x, 'alpha', [(d, d ^ k) for d in range(senders)])]
  transfers between devices with their start and end apart: 7 -> 7, of which waited for: 4 -> 4; matrix products, arithmetic and copies ran while one was open for 0% -> 0% of each run, Pallas kernels for 22% -> 20%
where the time goes in v3:
time: 24.2 us; the launch traced here: 24 us
  starting transfers between devices  9.29 us (38%)
  Pallas kernels  7.22 us (30%)
  waiting for transfers between devices  6.79 us (28%)
  other arithmetic  0.64 us (3%)
    ppermute x6, starting transfers between devices, exchange(): lax.ppermute(x, 'alpha', [(d, d ^ k) for d in range(senders)])  9.22 us
    ppermute x6, waiting for transfers between devices, exchange(): lax.ppermute(x, 'alpha', [(d, d ^ k) for d in range(senders)])  6.27 us
    pallas_call x1, Pallas kernels, on_device(): pl.pallas_call(lambda *refs: tables_kernel(beta_blocks, outer, inner, *re...  2.98 us
    pallas_call x1, Pallas kernels, on_device(): pl.pallas_call(lambda *refs: fetch_kernel(width, *refs), in_specs=[pl.Blo...  1.2 us
    pallas_call x1, Pallas kernels, on_device(): pl.pallas_call(lambda *refs: right_kernel(strings, width, inner, *refs),...  0.82 us
    pallas_call x1, Pallas kernels, on_device(): pl.pallas_call(pack_kernel, in_specs=[pl.BlockSpec(memory_space=pltpu.HBM...  0.79 us
    pallas_call x1, Pallas kernels, on_device(): pl.pallas_call(lambda *refs: forward_kernel(strings, width, local_rows, s...  0.72 us
    pallas_call x1, Pallas kernels, on_device(): pl.pallas_call(lambda *refs: sigma_kernel(strings, width, 0, *refs), out_...  0.71 us
  transfers between devices with their start and end apart: 7, of which 4 were waited for; matrix products, arithmetic and copies ran while one was open for 0% of the time, Pallas kernels for 20%

profile of v3, /device:TPU:0, one launch (start us, length us, event | category | flops | bytes accessed | tf_op | source)
XLA Modules:
  0.0 24.0 jit_solution(4847731555243786355)
XLA Ops:
  0.0 0.8 %pack.1.refs_0_.refs_7_ = bf16[80,256]{1,0:T(8,128)(2,1)S(1)} custom-call(bf16[64,256]{1,0:T(8,128)(2,1)} %coeffs_ref.1, s32[1,128]{1,0:T(1,128)} %send_ref.1), custom_call_target="tpu_custom_call" | custom-call | tf_op jit(solution)/shard_map/pack/pallas_call | solution.py:274
  0.8 4.1 %collective-permute-start.2 = (bf16[80,256]{1,0:T(8,128)(2,1)S(1)}, bf16[80,256]{1,0:T(8,128)(2,1)S(1)}, u32[]{:S(2)}, u32[]{:S(2)}) collective-permute-start(bf16[80,256]{1,0:T(8,128)(2,1)S(1)} %pack.1.refs_0_.refs_7_), channel_id=1, source_target_pairs={{0,16},{2,18},{4,20},{6,22},{8,24},{10,26},{12,28},{14,30},{16,0},... | collective-permute-start | bytes 122888 | tf_op jit(solution)/shard_map/ppermute | solution.py:269
  4.9 1.6 %collective-permute-start.1 = (bf16[80,256]{1,0:T(8,128)(2,1)S(1)}, bf16[80,256]{1,0:T(8,128)(2,1)S(1)}, u32[]{:S(2)}, u32[]{:S(2)}) collective-permute-start(bf16[80,256]{1,0:T(8,128)(2,1)S(1)} %pack.1.refs_0_.refs_7_), channel_id=1, source_target_pairs={{0,8},{2,10},{4,12},{6,14},{8,0},{10,2},{12,4},{14,6},{16,24},{18,... | collective-permute-start | bytes 122888 | tf_op jit(solution)/shard_map/ppermute | solution.py:269
  6.5 0.0 collective-permute-start
  6.5 1.2 %fetch.1 = (s32[16,132]{1,0:T(8,128)S(1)}, s32[16,132]{1,0:T(8,128)S(1)}, s32[16,132]{1,0:T(8,128)S(1)}, s32[16,132]{1,0:T(8,128)S(1)}, s32[16,132]{1,0:T(8,128)...) custom-call(s32[16,132]{1,0:T(8,128)} %refs_0_.1, s32[16,132]{1,0:T(8,128)} %refs_1_.1, ...), custom_call_target="tpu_custom_call" | custom-call | tf_op jit(solution)/shard_map/fetch/pallas_call | solution.py:290
  7.7 0.0 collective-permute-done.2.refs_3_
  7.7 1.2 %collective-permute-done.1.refs_2_ = bf16[80,256]{1,0:T(8,128)(2,1)S(1)} collective-permute-done((bf16[80,256]{1,0:T(8,128)(2,1)S(1)}, bf16[80,256]{1,0:T(8,128)(2,1)S(1)}, u32[]{:S(2)}, u32[]{:S(2)}) %collective-permute-start.1) | collective-permute-done | bytes 40992 | tf_op jit(solution)/shard_map/ppermute | solution.py:269
  8.9 3.4 %collective-permute-done.refs_1_ = bf16[80,256]{1,0:T(8,128)(2,1)S(1)} collective-permute-done((bf16[80,256]{1,0:T(8,128)(2,1)S(1)}, bf16[80,256]{1,0:T(8,128)(2,1)S(1)}, u32[]{:S(2)}, u32[]{:S(2)}) %collective-permute-start) | collective-permute-done | bytes 40992 | tf_op jit(solution)/shard_map/ppermute | solution.py:269
  12.3 0.7 %forward.1 = (bf16[32,1024]{1,0:T(8,128)(2,1)S(1)}, bf16[32,1024]{1,0:T(8,128)(2,1)S(1)}, bf16[32,1024]{1,0:T(8,128)(2,1)S(1)}, bf16[32,1024]{1,0:T(8,128)(2,1)S(1)}) custom-call(bf16[80,256]{1,0:T(8,128)(2,1)S(1)} %pack.1.refs_0_.refs_7_, bf16[80,256]{1,0:T(8,128)(2,1)S(1)} %collective-permute-done.refs_1_, ...), custom_call_target="tpu_custom_call" | custom-call | tf_op jit(solution)/shard_map/forward/pallas_call | solution.py:300
  13.0 1.5 %collective-permute-start.3 = (bf16[32,1024]{1,0:T(8,128)(2,1)S(1)}, bf16[32,1024]{1,0:T(8,128)(2,1)S(1)}, u32[]{:S(2)}, u32[]{:S(2)}) collective-permute-start(bf16[32,1024]{1,0:T(8,128)(2,1)S(1)} %get-tuple-element.20), channel_id=1, source_target_pairs={{0,2},{2,0},{4,6},{6,4},{8,10},{10,8},{12,14},{14,12},{16,18},{18,... | collective-permute-start | bytes 196616 | tf_op jit(solution)/shard_map/ppermute | solution.py:269
  14.5 1.5 %collective-permute-start.4 = (bf16[32,1024]{1,0:T(8,128)(2,1)S(1)}, bf16[32,1024]{1,0:T(8,128)(2,1)S(1)}, u32[]{:S(2)}, u32[]{:S(2)}) collective-permute-start(bf16[32,1024]{1,0:T(8,128)(2,1)S(1)} %get-tuple-element.21), channel_id=1, source_target_pairs={{0,4},{2,6},{4,0},{6,2},{8,12},{10,14},{12,8},{14,10},{16,20},{18,... | collective-permute-start | bytes 196616 | tf_op jit(solution)/shard_map/ppermute | solution.py:269
  16.1 0.5 %collective-permute-start.5 = (bf16[32,1024]{1,0:T(8,128)(2,1)S(1)}, bf16[32,1024]{1,0:T(8,128)(2,1)S(1)}, u32[]{:S(2)}, u32[]{:S(2)}) collective-permute-start(bf16[32,1024]{1,0:T(8,128)(2,1)S(1)} %get-tuple-element.22), channel_id=1, source_target_pairs={{0,6},{2,4},{4,2},{6,0},{8,14},{10,12},{12,10},{14,8},{16,22},{18,... | collective-permute-start | bytes 196616 | tf_op jit(solution)/shard_map/ppermute | solution.py:269
  16.5 3.0 %tables.1.refs_4_.refs_1_ = bf16[256,4096]{1,0:T(8,128)(2,1)S(1)} custom-call(s32[16,132]{1,0:T(8,128)S(1)} %get-tuple-element.23.refs_0_, s32[16,132]{1,0:T(8,128)S(1)} %get-tuple-element.24.refs_1_, s32[16,132]{1,0:T(8,128)S(1)} %get-tuple-element.25.refs_2_, s32[16,132]{1,0:T(8,128)S(1)} %get-tuple-element.26.refs_3_, ...), custom_call_target="tpu_custom_call" | custom-call | flops 1254899712 | bytes 8388608 | tf_op jit(solution)/shard_map/tables/pallas_call | solution.py:308
  19.5 0.0 collective-permute-done.3.refs_1_
  19.5 0.0 collective-permute-done.4.refs_2_
  19.5 1.7 %collective-permute-done.5.refs_3_ = bf16[32,1024]{1,0:T(8,128)(2,1)S(1)} collective-permute-done((bf16[32,1024]{1,0:T(8,128)(2,1)S(1)}, bf16[32,1024]{1,0:T(8,128)(2,1)S(1)}, u32[]{:S(2)}, u32[]{:S(2)}) %collective-permute-start.5) | collective-permute-done | bytes 65568 | tf_op jit(solution)/shard_map/ppermute | solution.py:269
  21.2 0.8 %theirs.1 = (bf16[4096,128]{1,0:T(8,128)(2,1)S(1)}, f32[64,256]{1,0:T(8,128)S(1)}) custom-call(bf16[32,1024]{1,0:T(8,128)(2,1)S(1)} %get-tuple-element.19.refs_7_.refs_0_, bf16[32,1024]{1,0:T(8,128)(2,1)S(1)} %collective-permute-done.3.refs_1_, bf16[32,1024]{1,0:T(8,128)(2,1)S(1)} %collective-permute-done.4.refs_2_, ...), custom_call_target="tpu_custom_call" | custom-call | flops 134217728 | bytes 3145728 | tf_op jit(solution)/shard_map/theirs/pallas_call | solution.py:336
  22.0 0.1 collective-permute-start.6
  22.1 0.7 %mine.1 = f32[64,256]{1,0:T(8,128)S(1)} custom-call(bf16[4096,128]{1,0:T(8,128)(2,1)S(1)} %get-tuple-element.31.refs_0_, bf16[256,4096]{1,0:T(8,128)(2,1)S(1)} %tables.1.refs_4_.refs_1_, bf16[256,1024]{1,0:T(8,128)(2,1)S(1)} %get-tuple-element.30.refs_5_.refs_2_), custom_call_target="tpu_custom_call" | custom-call | flops 134217728 | bytes 3145728 | tf_op jit(solution)/shard_map/mine/pallas_call | solution.py:355
  22.8 0.5 %collective-permute-done.6 = f32[64,256]{1,0:T(8,128)S(1)} collective-permute-done((f32[64,256]{1,0:T(8,128)S(1)}, f32[64,256]{1,0:T(8,128)S(1)}, u32[]{:S(2)}, u32[]{:S(2)}) %collective-permute-start.6) | collective-permute-done | bytes 65568 | tf_op jit(solution)/shard_map/ppermute | solution.py:346
  23.4 0.6 %add.3 = f32[64,256]{1,0:T(8,128)} add(f32[64,256]{1,0:T(8,128)S(1)} %mine.1, f32[64,256]{1,0:T(8,128)S(1)} %collective-permute-done.6) | non-fusion elementwise | flops 16384 | bytes 196608 | tf_op jit(solution)/shard_map/add | solution.py:359
Async XLA Ops:
  0.8 6.9 %collective-permute-start.2 = (bf16[80,256]{1,0:T(8,128)(2,1)S(1)}, bf16[80,256]{1,0:T(8,128)(2,1)S(1)}, u32[]{:S(2)}, u32[]{:S(2)}) collective-permute-start(bf16[80,256]{1,0:T(8,128)(2,1)S(1)} %pack.1.refs_0_.refs_7_), channel_id=1, source_target_pairs={{0,16},{2,18},{4,20},{6,22},{8,24},{10,26},{12,28},{14,30},{16,0},... | collective-permute-start | bytes 122888 | tf_op jit(solution)/shard_map/ppermute | solution.py:269
  4.9 4.0 %collective-permute-start.1 = (bf16[80,256]{1,0:T(8,128)(2,1)S(1)}, bf16[80,256]{1,0:T(8,128)(2,1)S(1)}, u32[]{:S(2)}, u32[]{:S(2)}) collective-permute-start(bf16[80,256]{1,0:T(8,128)(2,1)S(1)} %pack.1.refs_0_.refs_7_), channel_id=1, source_target_pairs={{0,8},{2,10},{4,12},{6,14},{8,0},{10,2},{12,4},{14,6},{16,24},{18,... | collective-permute-start | bytes 122888 | tf_op jit(solution)/shard_map/ppermute | solution.py:269
  6.5 5.8 %collective-permute-start = (bf16[80,256]{1,0:T(8,128)(2,1)S(1)}, bf16[80,256]{1,0:T(8,128)(2,1)S(1)}, u32[]{:S(2)}, u32[]{:S(2)}) collective-permute-start(bf16[80,256]{1,0:T(8,128)(2,1)S(1)} %pack.1.refs_0_.refs_7_), channel_id=1, source_target_pairs={{0,24},{2,26},{4,28},{6,30},{8,16},{10,18},{12,20},{14,22},{16,8},... | collective-permute-start | bytes 122888 | tf_op jit(solution)/shard_map/ppermute | solution.py:269
  13.0 6.5 %collective-permute-start.3 = (bf16[32,1024]{1,0:T(8,128)(2,1)S(1)}, bf16[32,1024]{1,0:T(8,128)(2,1)S(1)}, u32[]{:S(2)}, u32[]{:S(2)}) collective-permute-start(bf16[32,1024]{1,0:T(8,128)(2,1)S(1)} %get-tuple-element.20), channel_id=1, source_target_pairs={{0,2},{2,0},{4,6},{6,4},{8,10},{10,8},{12,14},{14,12},{16,18},{18,... | collective-permute-start | bytes 196616 | tf_op jit(solution)/shard_map/ppermute | solution.py:269
  14.5 5.0 %collective-permute-start.4 = (bf16[32,1024]{1,0:T(8,128)(2,1)S(1)}, bf16[32,1024]{1,0:T(8,128)(2,1)S(1)}, u32[]{:S(2)}, u32[]{:S(2)}) collective-permute-start(bf16[32,1024]{1,0:T(8,128)(2,1)S(1)} %get-tuple-element.21), channel_id=1, source_target_pairs={{0,4},{2,6},{4,0},{6,2},{8,12},{10,14},{12,8},{14,10},{16,20},{18,... | collective-permute-start | bytes 196616 | tf_op jit(solution)/shard_map/ppermute | solution.py:269
  16.1 5.2 %collective-permute-start.5 = (bf16[32,1024]{1,0:T(8,128)(2,1)S(1)}, bf16[32,1024]{1,0:T(8,128)(2,1)S(1)}, u32[]{:S(2)}, u32[]{:S(2)}) collective-permute-start(bf16[32,1024]{1,0:T(8,128)(2,1)S(1)} %get-tuple-element.22), channel_id=1, source_target_pairs={{0,6},{2,4},{4,2},{6,0},{8,14},{10,12},{12,10},{14,8},{16,22},{18,... | collective-permute-start | bytes 196616 | tf_op jit(solution)/shard_map/ppermute | solution.py:269
  22.0 1.3 %collective-permute-start.6 = (f32[64,256]{1,0:T(8,128)S(1)}, f32[64,256]{1,0:T(8,128)S(1)}, u32[]{:S(2)}, u32[]{:S(2)}) collective-permute-start(f32[64,256]{1,0:T(8,128)S(1)} %get-tuple-element.32), channel_id=1, source_target_pairs={{0,1},{1,0},{2,3},{3,2},{4,5},{5,4},{6,7},{7,6},{8,9},{9,8},{10,11... | collective-permute-start | bytes 196616 | tf_op jit(solution)/shard_map/ppermute | solution.py:346

commit v4 on v2

--- a/solution.py
+++ b/solution.py
@@ -183,9 +183,9 @@
                     out_ref[rows, first + slots : first + 2 * slots] = low[source, lanes]
 
 
-def right_kernel(strings, width, inner, *refs):
+def right_kernel(strings, width, inner, turn, *refs):
     received_refs, (table_ref, expand_ref, right_ref), rest = refs[:inner], refs[inner : inner + 3], refs[inner + 3 :]
-    received = jnp.concatenate([ref[...] for ref in received_refs], axis=0)
+    received = jnp.concatenate([received_refs[turn.index(j)][...] for j in range(inner)], axis=0)
     slots, wide = received.shape
     group = strings * width
     both = BATCHES * group
@@ -301,6 +301,7 @@
         name="forward",
     )(*gathered)
     received = [exchange(x, j) for j, x in enumerate(outgoing)]
+    turn = sorted(range(inner), key=lambda j: -format(j or outer * inner * 2 - 1, "b").count("1"))
     flops = 2 * beta_local * beta_blocks * orbitals * (orbitals + 2 * pairs * slots)
     table = pl.pallas_call(
         lambda *refs: tables_kernel(beta_blocks, outer, inner, *refs),
@@ -331,11 +332,11 @@
         ),
     )
     right, theirs = pl.pallas_call(
-        lambda *refs: right_kernel(strings, width, inner, *refs),
+        lambda *refs: right_kernel(strings, width, inner, turn, *refs),
         out_shape=[jax.ShapeDtypeStruct((2 * beta_local * slots, both), BF), part],
         name="theirs",
         **call,
-    )(*received, table, expand)
+    )(*(received[j] for j in turn), table, expand)
 
     def route(step):
         return [(core, (core + step) % cores) for core in range(cores)]

time: 22.8 us -> 21.9 us (0.961)
  waiting for transfers between devices: 5.26 us -> 4.35 us
    ppermute x6, waiting for transfers between devices: 4.74 us -> 3.82 us  [exchange(): lax.ppermute(x, 'alpha', [(d, d ^ k) for d in range(senders)])]
  transfers between devices with their start and end apart: 7 -> 7, of which waited for: 4 -> 5; matrix products, arithmetic and copies ran while one was open for 0% -> 0% of each run, Pallas kernels for 22% -> 23%
where the time goes in v4:
time: 21.9 us; the launch traced here: 21.6 us
  starting transfers between devices  9.36 us (43%)
  Pallas kernels  7.24 us (33%)
  waiting for transfers between devices  4.35 us (20%)
  other arithmetic  0.64 us (3%)
    ppermute x6, starting transfers between devices, exchange(): lax.ppermute(x, 'alpha', [(d, d ^ k) for d in range(senders)])  9.3 us
    ppermute x6, waiting for transfers between devices, exchange(): lax.ppermute(x, 'alpha', [(d, d ^ k) for d in range(senders)])  3.82 us
    pallas_call x1, Pallas kernels, on_device(): pl.pallas_call(lambda *refs: tables_kernel(beta_blocks, outer, inner, *re...  2.98 us
    pallas_call x1, Pallas kernels, on_device(): pl.pallas_call(lambda *refs: fetch_kernel(width, *refs), in_specs=[pl.Blo...  1.2 us
    pallas_call x1, Pallas kernels, on_device(): pl.pallas_call(lambda *refs: right_kernel(strings, width, inner, turn, *r...  0.85 us
    pallas_call x1, Pallas kernels, on_device(): pl.pallas_call(pack_kernel, in_specs=[pl.BlockSpec(memory_space=pltpu.HBM...  0.79 us
    pallas_call x1, Pallas kernels, on_device(): pl.pallas_call(lambda *refs: sigma_kernel(strings, width, 0, *refs), out_...  0.71 us
    pallas_call x1, Pallas kernels, on_device(): pl.pallas_call(lambda *refs: forward_kernel(strings, width, local_rows, s...  0.71 us
  transfers between devices with their start and end apart: 7, of which 5 were waited for; matrix products, arithmetic and copies ran while one was open for 0% of the time, Pallas kernels for 23%

profile of v4, /device:TPU:0, one launch (start us, length us, event | category | flops | bytes accessed | tf_op | source)
XLA Modules:
  0.0 21.6 jit_solution(6022455329233691328)
XLA Ops:
  0.0 0.8 %pack.1.refs_0_.refs_7_ = bf16[80,256]{1,0:T(8,128)(2,1)S(1)} custom-call(bf16[64,256]{1,0:T(8,128)(2,1)} %coeffs_ref.1, s32[1,128]{1,0:T(1,128)} %send_ref.1), custom_call_target="tpu_custom_call" | custom-call | tf_op jit(solution)/shard_map/pack/pallas_call | solution.py:274
  0.8 5.1 %collective-permute-start.2 = (bf16[80,256]{1,0:T(8,128)(2,1)S(1)}, bf16[80,256]{1,0:T(8,128)(2,1)S(1)}, u32[]{:S(2)}, u32[]{:S(2)}) collective-permute-start(bf16[80,256]{1,0:T(8,128)(2,1)S(1)} %pack.1.refs_0_.refs_7_), channel_id=1, source_target_pairs={{0,24},{2,26},{4,28},{6,30},{8,16},{10,18},{12,20},{14,22},{16,8},... | collective-permute-start | bytes 122888 | tf_op jit(solution)/shard_map/ppermute | solution.py:269
  5.9 0.0 collective-permute-start.1
  5.9 0.6 %collective-permute-start = (bf16[80,256]{1,0:T(8,128)(2,1)S(1)}, bf16[80,256]{1,0:T(8,128)(2,1)S(1)}, u32[]{:S(2)}, u32[]{:S(2)}) collective-permute-start(bf16[80,256]{1,0:T(8,128)(2,1)S(1)} %pack.1.refs_0_.refs_7_), channel_id=1, source_target_pairs={{0,8},{2,10},{4,12},{6,14},{8,0},{10,2},{12,4},{14,6},{16,24},{18,... | collective-permute-start | bytes 122888 | tf_op jit(solution)/shard_map/ppermute | solution.py:269
  6.6 1.2 %fetch.1 = (s32[16,132]{1,0:T(8,128)S(1)}, s32[16,132]{1,0:T(8,128)S(1)}, s32[16,132]{1,0:T(8,128)S(1)}, s32[16,132]{1,0:T(8,128)S(1)}, s32[16,132]{1,0:T(8,128)...) custom-call(s32[16,132]{1,0:T(8,128)} %refs_0_.1, s32[16,132]{1,0:T(8,128)} %refs_1_.1, ...), custom_call_target="tpu_custom_call" | custom-call | tf_op jit(solution)/shard_map/fetch/pallas_call | solution.py:287
  7.8 0.2 collective-permute-done.2.refs_3_
  7.9 2.9 %collective-permute-done.1.refs_2_ = bf16[80,256]{1,0:T(8,128)(2,1)S(1)} collective-permute-done((bf16[80,256]{1,0:T(8,128)(2,1)S(1)}, bf16[80,256]{1,0:T(8,128)(2,1)S(1)}, u32[]{:S(2)}, u32[]{:S(2)}) %collective-permute-start.1) | collective-permute-done | bytes 40992 | tf_op jit(solution)/shard_map/ppermute | solution.py:269
  10.8 0.0 collective-permute-done.refs_1_
  10.8 0.7 %forward.1 = (bf16[32,1024]{1,0:T(8,128)(2,1)S(1)}, bf16[32,1024]{1,0:T(8,128)(2,1)S(1)}, bf16[32,1024]{1,0:T(8,128)(2,1)S(1)}, bf16[32,1024]{1,0:T(8,128)(2,1)S(1)}) custom-call(bf16[80,256]{1,0:T(8,128)(2,1)S(1)} %pack.1.refs_0_.refs_7_, bf16[80,256]{1,0:T(8,128)(2,1)S(1)} %collective-permute-done.refs_1_, ...), custom_call_target="tpu_custom_call" | custom-call | tf_op jit(solution)/shard_map/forward/pallas_call | solution.py:297
  11.5 2.5 %collective-permute-start.3 = (bf16[32,1024]{1,0:T(8,128)(2,1)S(1)}, bf16[32,1024]{1,0:T(8,128)(2,1)S(1)}, u32[]{:S(2)}, u32[]{:S(2)}) collective-permute-start(bf16[32,1024]{1,0:T(8,128)(2,1)S(1)} %get-tuple-element.20), channel_id=1, source_target_pairs={{0,6},{2,4},{4,2},{6,0},{8,14},{10,12},{12,10},{14,8},{16,22},{18,... | collective-permute-start | bytes 196616 | tf_op jit(solution)/shard_map/ppermute | solution.py:269
  14.0 0.5 %collective-permute-start.4 = (bf16[32,1024]{1,0:T(8,128)(2,1)S(1)}, bf16[32,1024]{1,0:T(8,128)(2,1)S(1)}, u32[]{:S(2)}, u32[]{:S(2)}) collective-permute-start(bf16[32,1024]{1,0:T(8,128)(2,1)S(1)} %get-tuple-element.21), channel_id=1, source_target_pairs={{0,2},{2,0},{4,6},{6,4},{8,10},{10,8},{12,14},{14,12},{16,18},{18,... | collective-permute-start | bytes 196616 | tf_op jit(solution)/shard_map/ppermute | solution.py:269
  14.6 0.5 %collective-permute-start.5 = (bf16[32,1024]{1,0:T(8,128)(2,1)S(1)}, bf16[32,1024]{1,0:T(8,128)(2,1)S(1)}, u32[]{:S(2)}, u32[]{:S(2)}) collective-permute-start(bf16[32,1024]{1,0:T(8,128)(2,1)S(1)} %get-tuple-element.22), channel_id=1, source_target_pairs={{0,4},{2,6},{4,0},{6,2},{8,12},{10,14},{12,8},{14,10},{16,20},{18,... | collective-permute-start | bytes 196616 | tf_op jit(solution)/shard_map/ppermute | solution.py:269
  15.1 3.0 %tables.1.refs_4_.refs_1_ = bf16[256,4096]{1,0:T(8,128)(2,1)S(1)} custom-call(s32[16,132]{1,0:T(8,128)S(1)} %get-tuple-element.23.refs_0_, s32[16,132]{1,0:T(8,128)S(1)} %get-tuple-element.24.refs_1_, s32[16,132]{1,0:T(8,128)S(1)} %get-tuple-element.25.refs_2_, s32[16,132]{1,0:T(8,128)S(1)} %get-tuple-element.26.refs_3_, ...), custom_call_target="tpu_custom_call" | custom-call | flops 1254899712 | bytes 8388608 | tf_op jit(solution)/shard_map/tables/pallas_call | solution.py:306
  18.1 0.0 collective-permute-done.3.refs_1_
  18.1 0.2 %collective-permute-done.4.refs_2_ = bf16[32,1024]{1,0:T(8,128)(2,1)S(1)} collective-permute-done((bf16[32,1024]{1,0:T(8,128)(2,1)S(1)}, bf16[32,1024]{1,0:T(8,128)(2,1)S(1)}, u32[]{:S(2)}, u32[]{:S(2)}) %collective-permute-start.4) | collective-permute-done | bytes 65568 | tf_op jit(solution)/shard_map/ppermute | solution.py:269
  18.3 0.5 %collective-permute-done.5.refs_3_ = bf16[32,1024]{1,0:T(8,128)(2,1)S(1)} collective-permute-done((bf16[32,1024]{1,0:T(8,128)(2,1)S(1)}, bf16[32,1024]{1,0:T(8,128)(2,1)S(1)}, u32[]{:S(2)}, u32[]{:S(2)}) %collective-permute-start.5) | collective-permute-done | bytes 65568 | tf_op jit(solution)/shard_map/ppermute | solution.py:269
  18.8 0.8 %theirs.1 = (bf16[4096,128]{1,0:T(8,128)(2,1)S(1)}, f32[64,256]{1,0:T(8,128)S(1)}) custom-call(bf16[32,1024]{1,0:T(8,128)(2,1)S(1)} %get-tuple-element.19.refs_7_.refs_0_, bf16[32,1024]{1,0:T(8,128)(2,1)S(1)} %collective-permute-done.3.refs_1_, bf16[32,1024]{1,0:T(8,128)(2,1)S(1)} %collective-permute-done.4.refs_2_, ...), custom_call_target="tpu_custom_call" | custom-call | flops 134217728 | bytes 3145728 | tf_op jit(solution)/shard_map/theirs/pallas_call | solution.py:334
  19.7 0.1 collective-permute-start.6
  19.8 0.7 %mine.1 = f32[64,256]{1,0:T(8,128)S(1)} custom-call(bf16[4096,128]{1,0:T(8,128)(2,1)S(1)} %get-tuple-element.31.refs_0_, bf16[256,4096]{1,0:T(8,128)(2,1)S(1)} %tables.1.refs_4_.refs_1_, bf16[256,1024]{1,0:T(8,128)(2,1)S(1)} %get-tuple-element.30.refs_5_.refs_2_), custom_call_target="tpu_custom_call" | custom-call | flops 134217728 | bytes 3145728 | tf_op jit(solution)/shard_map/mine/pallas_call | solution.py:353
  20.5 0.5 %collective-permute-done.6 = f32[64,256]{1,0:T(8,128)S(1)} collective-permute-done((f32[64,256]{1,0:T(8,128)S(1)}, f32[64,256]{1,0:T(8,128)S(1)}, u32[]{:S(2)}, u32[]{:S(2)}) %collective-permute-start.6) | collective-permute-done | bytes 65568 | tf_op jit(solution)/shard_map/ppermute | solution.py:344
  21.0 0.6 %add.3 = f32[64,256]{1,0:T(8,128)} add(f32[64,256]{1,0:T(8,128)S(1)} %mine.1, f32[64,256]{1,0:T(8,128)S(1)} %collective-permute-done.6) | non-fusion elementwise | flops 16384 | bytes 196608 | tf_op jit(solution)/shard_map/add | solution.py:357
Async XLA Ops:
  0.8 7.1 %collective-permute-start.2 = (bf16[80,256]{1,0:T(8,128)(2,1)S(1)}, bf16[80,256]{1,0:T(8,128)(2,1)S(1)}, u32[]{:S(2)}, u32[]{:S(2)}) collective-permute-start(bf16[80,256]{1,0:T(8,128)(2,1)S(1)} %pack.1.refs_0_.refs_7_), channel_id=1, source_target_pairs={{0,24},{2,26},{4,28},{6,30},{8,16},{10,18},{12,20},{14,22},{16,8},... | collective-permute-start | bytes 122888 | tf_op jit(solution)/shard_map/ppermute | solution.py:269
  5.9 4.9 %collective-permute-start.1 = (bf16[80,256]{1,0:T(8,128)(2,1)S(1)}, bf16[80,256]{1,0:T(8,128)(2,1)S(1)}, u32[]{:S(2)}, u32[]{:S(2)}) collective-permute-start(bf16[80,256]{1,0:T(8,128)(2,1)S(1)} %pack.1.refs_0_.refs_7_), channel_id=1, source_target_pairs={{0,16},{2,18},{4,20},{6,22},{8,24},{10,26},{12,28},{14,30},{16,0},... | collective-permute-start | bytes 122888 | tf_op jit(solution)/shard_map/ppermute | solution.py:269
  5.9 4.9 %collective-permute-start = (bf16[80,256]{1,0:T(8,128)(2,1)S(1)}, bf16[80,256]{1,0:T(8,128)(2,1)S(1)}, u32[]{:S(2)}, u32[]{:S(2)}) collective-permute-start(bf16[80,256]{1,0:T(8,128)(2,1)S(1)} %pack.1.refs_0_.refs_7_), channel_id=1, source_target_pairs={{0,8},{2,10},{4,12},{6,14},{8,0},{10,2},{12,4},{14,6},{16,24},{18,... | collective-permute-start | bytes 122888 | tf_op jit(solution)/shard_map/ppermute | solution.py:269
  11.5 6.5 %collective-permute-start.3 = (bf16[32,1024]{1,0:T(8,128)(2,1)S(1)}, bf16[32,1024]{1,0:T(8,128)(2,1)S(1)}, u32[]{:S(2)}, u32[]{:S(2)}) collective-permute-start(bf16[32,1024]{1,0:T(8,128)(2,1)S(1)} %get-tuple-element.20), channel_id=1, source_target_pairs={{0,6},{2,4},{4,2},{6,0},{8,14},{10,12},{12,10},{14,8},{16,22},{18,... | collective-permute-start | bytes 196616 | tf_op jit(solution)/shard_map/ppermute | solution.py:269
  14.0 4.3 %collective-permute-start.4 = (bf16[32,1024]{1,0:T(8,128)(2,1)S(1)}, bf16[32,1024]{1,0:T(8,128)(2,1)S(1)}, u32[]{:S(2)}, u32[]{:S(2)}) collective-permute-start(bf16[32,1024]{1,0:T(8,128)(2,1)S(1)} %get-tuple-element.21), channel_id=1, source_target_pairs={{0,2},{2,0},{4,6},{6,4},{8,10},{10,8},{12,14},{14,12},{16,18},{18,... | collective-permute-start | bytes 196616 | tf_op jit(solution)/shard_map/ppermute | solution.py:269
  14.6 4.3 %collective-permute-start.5 = (bf16[32,1024]{1,0:T(8,128)(2,1)S(1)}, bf16[32,1024]{1,0:T(8,128)(2,1)S(1)}, u32[]{:S(2)}, u32[]{:S(2)}) collective-permute-start(bf16[32,1024]{1,0:T(8,128)(2,1)S(1)} %get-tuple-element.22), channel_id=1, source_target_pairs={{0,4},{2,6},{4,0},{6,2},{8,12},{10,14},{12,8},{14,10},{16,20},{18,... | collective-permute-start | bytes 196616 | tf_op jit(solution)/shard_map/ppermute | solution.py:269
  19.7 1.3 %collective-permute-start.6 = (f32[64,256]{1,0:T(8,128)S(1)}, f32[64,256]{1,0:T(8,128)S(1)}, u32[]{:S(2)}, u32[]{:S(2)}) collective-permute-start(f32[64,256]{1,0:T(8,128)S(1)} %get-tuple-element.32), channel_id=1, source_target_pairs={{0,1},{1,0},{2,3},{3,2},{4,5},{5,4},{6,7},{7,6},{8,9},{9,8},{10,11... | collective-permute-start | bytes 196616 | tf_op jit(solution)/shard_map/ppermute | solution.py:344

commit v5 on v4

--- a/solution.py
+++ b/solution.py
@@ -72,8 +72,8 @@
 
 
 def fetch_kernel(width, *refs):
-    count = (len(refs) - 3) // 2
-    expand_ref, sems = refs[-2:]
+    count = (len(refs) - 4) // 2
+    expand_ref, spread_ref, sems = refs[-3:]
     moves = [
         pltpu.make_async_copy(refs[i], refs[count + 1 + i], sems.at[i]) for i in range(count)
     ]
@@ -84,12 +84,16 @@
     expand_ref[...] = one(
         modulo(column_of(rows), rows // 2) == over(n, LANES) * width + modulo(n, width)
     )
+    rows, columns = spread_ref.shape
+    n = row_of(columns)
+    group = columns // rows * width
+    spread_ref[...] = one(column_of(rows) == over(n, group) * width + modulo(n, width))
     for move in moves:
         move.wait()
 
 
 def forward_kernel(strings, width, rows, slots, outer, *refs):
-    gathered_refs, out_refs = refs[:outer], refs[outer:]
+    gathered_refs, spread_ref, out_refs = refs[:outer], refs[outer], refs[outer + 1 :]
     inner = len(out_refs)
     columns = gathered_refs[0].shape[1]
     wide = strings * columns
@@ -97,10 +101,9 @@
     per = BATCHES * CAP
     blocks = rows // strings
     n = row_of(wide)
-    spread = one(column_of(columns) == over(n, group) * width + modulo(n, width))
     gathered = jnp.concatenate([ref[:rows, :] for ref in gathered_refs], axis=0)
     keep = modulo(column_of(outer * rows), strings) == modulo(over(n, width), strings)
-    spaced = jnp.where(keep, dot(gathered, spread), 0.0).astype(BF)
+    spaced = jnp.where(keep, dot(gathered, spread_ref[...]), 0.0).astype(BF)
     r = column_of(inner * per)
     receiver = over(r, per) ^ lax.axis_index("alpha")
     wanted = over(modulo(r, per), CAP) * (slots // BATCHES) + receiver * CAP + modulo(r, CAP)
@@ -284,12 +287,15 @@
     )(*pinned(coeffs, send_block))
     gathered = [exchange(packed, k * inner) for k in range(outer)]
     both = BATCHES * strings * width
-    *tables, expand = pl.pallas_call(
+    *tables, expand, spread = pl.pallas_call(
         lambda *refs: fetch_kernel(width, *refs),
         in_specs=[pl.BlockSpec(memory_space=pltpu.HBM)] * len(others)
         + [pl.BlockSpec(memory_space=pl.ANY)],
         out_shape=[jax.ShapeDtypeStruct(x.shape, x.dtype) for x in others]
-        + [jax.ShapeDtypeStruct((2 * both, BATCHES * strings * LANES), BF)],
+        + [
+            jax.ShapeDtypeStruct((2 * both, BATCHES * strings * LANES), BF),
+            jax.ShapeDtypeStruct((local_columns, wide), BF),
+        ],
         scratch_shapes=[pltpu.SemaphoreType.DMA((len(others),))],
         compiler_params=pltpu.CompilerParams(vmem_limit_bytes=40 * 2**20),
         name="fetch",
@@ -299,9 +305,10 @@
         out_shape=[jax.ShapeDtypeStruct((outer * per, wide), BF)] * inner,
         compiler_params=pltpu.CompilerParams(vmem_limit_bytes=40 * 2**20),
         name="forward",
-    )(*gathered)
+    )(*gathered, spread)
     received = [exchange(x, j) for j, x in enumerate(outgoing)]
     turn = sorted(range(inner), key=lambda j: -format(j or outer * inner * 2 - 1, "b").count("1"))
+    turn = turn[:1] + turn[-2:-1] + turn[1:-2] + turn[-1:]
     flops = 2 * beta_local * beta_blocks * orbitals * (orbitals + 2 * pairs * slots)
     table = pl.pallas_call(
         lambda *refs: tables_kernel(beta_blocks, outer, inner, *refs),

time: 21.9 us -> 22 us (level)
  transfers between devices with their start and end apart: 7 -> 7, of which waited for: 5 -> 5; matrix products, arithmetic and copies ran while one was open for 0% -> 0% of each run, Pallas kernels for 23% -> 22%
where the time goes in v5:
time: 22 us; the launch traced here: 21.7 us
  starting transfers between devices  9.36 us (43%)
  Pallas kernels  7.2 us (33%)
  waiting for transfers between devices  4.46 us (20%)
  other arithmetic  0.64 us (3%)
    ppermute x6, starting transfers between devices, exchange(): lax.ppermute(x, 'alpha', [(d, d ^ k) for d in range(senders)])  9.3 us
    ppermute x6, waiting for transfers between devices, exchange(): lax.ppermute(x, 'alpha', [(d, d ^ k) for d in range(senders)])  3.92 us
    pallas_call x1, Pallas kernels, on_device(): pl.pallas_call(lambda *refs: tables_kernel(beta_blocks, outer, inner, *re...  2.98 us
    pallas_call x1, Pallas kernels, on_device(): pl.pallas_call(lambda *refs: fetch_kernel(width, *refs), in_specs=[pl.Blo...  1.2 us
    pallas_call x1, Pallas kernels, on_device(): pl.pallas_call(lambda *refs: right_kernel(strings, width, inner, turn, *r...  0.83 us
    pallas_call x1, Pallas kernels, on_device(): pl.pallas_call(pack_kernel, in_specs=[pl.BlockSpec(memory_space=pltpu.HBM...  0.79 us
    pallas_call x1, Pallas kernels, on_device(): pl.pallas_call(lambda *refs: forward_kernel(strings, width, local_rows, s...  0.7 us
    pallas_call x1, Pallas kernels, on_device(): pl.pallas_call(lambda *refs: sigma_kernel(strings, width, 0, *refs), out_...  0.7 us
  transfers between devices with their start and end apart: 7, of which 5 were waited for; matrix products, arithmetic and copies ran while one was open for 0% of the time, Pallas kernels for 22%

profile of v5, /device:TPU:0, one launch (start us, length us, event | category | flops | bytes accessed | tf_op | source)
XLA Modules:
  0.0 21.7 jit_solution(2917629113979250503)
XLA Ops:
  0.0 0.8 %pack.1.refs_7_.refs_0_ = bf16[80,256]{1,0:T(8,128)(2,1)S(1)} custom-call(bf16[64,256]{1,0:T(8,128)(2,1)} %coeffs_ref.1, s32[1,128]{1,0:T(1,128)} %send_ref.1), custom_call_target="tpu_custom_call" | custom-call | tf_op jit(solution)/shard_map/pack/pallas_call | solution.py:277
  0.8 5.1 %collective-permute-start.2 = (bf16[80,256]{1,0:T(8,128)(2,1)S(1)}, bf16[80,256]{1,0:T(8,128)(2,1)S(1)}, u32[]{:S(2)}, u32[]{:S(2)}) collective-permute-start(bf16[80,256]{1,0:T(8,128)(2,1)S(1)} %pack.1.refs_7_.refs_0_), channel_id=1, source_target_pairs={{0,24},{2,26},{4,28},{6,30},{8,16},{10,18},{12,20},{14,22},{16,8},... | collective-permute-start | bytes 122888 | tf_op jit(solution)/shard_map/ppermute | solution.py:272
  5.9 0.0 collective-permute-start.1
  5.9 0.6 %collective-permute-start = (bf16[80,256]{1,0:T(8,128)(2,1)S(1)}, bf16[80,256]{1,0:T(8,128)(2,1)S(1)}, u32[]{:S(2)}, u32[]{:S(2)}) collective-permute-start(bf16[80,256]{1,0:T(8,128)(2,1)S(1)} %pack.1.refs_7_.refs_0_), channel_id=1, source_target_pairs={{0,8},{2,10},{4,12},{6,14},{8,0},{10,2},{12,4},{14,6},{16,24},{18,... | collective-permute-start | bytes 122888 | tf_op jit(solution)/shard_map/ppermute | solution.py:272
  6.6 1.2 %fetch.1 = (s32[16,132]{1,0:T(8,128)S(1)}, s32[16,132]{1,0:T(8,128)S(1)}, s32[16,132]{1,0:T(8,128)S(1)}, s32[16,132]{1,0:T(8,128)S(1)}, s32[16,132]{1,0:T(8,128)...) custom-call(s32[16,132]{1,0:T(8,128)} %refs_0_.1, ...), custom_call_target="tpu_custom_call" | custom-call | tf_op jit(solution)/shard_map/fetch/pallas_call | solution.py:290
  7.8 0.2 collective-permute-done.2.refs_3_
  7.9 2.9 %collective-permute-done.1.refs_2_ = bf16[80,256]{1,0:T(8,128)(2,1)S(1)} collective-permute-done((bf16[80,256]{1,0:T(8,128)(2,1)S(1)}, bf16[80,256]{1,0:T(8,128)(2,1)S(1)}, u32[]{:S(2)}, u32[]{:S(2)}) %collective-permute-start.1) | collective-permute-done | bytes 40992 | tf_op jit(solution)/shard_map/ppermute | solution.py:272
  10.8 0.0 collective-permute-done.refs_1_
  10.8 0.7 %forward.1 = (bf16[32,1024]{1,0:T(8,128)(2,1)S(1)}, bf16[32,1024]{1,0:T(8,128)(2,1)S(1)}, bf16[32,1024]{1,0:T(8,128)(2,1)S(1)}, bf16[32,1024]{1,0:T(8,128)(2,1)S(1)}) custom-call(bf16[80,256]{1,0:T(8,128)(2,1)S(1)} %pack.1.refs_7_.refs_0_, bf16[80,256]{1,0:T(8,128)(2,1)S(1)} %collective-permute-done.refs_1_, ...), custom_call_target="tpu_custom_call" | custom-call | tf_op jit(solution)/shard_map/forward/pallas_call | solution.py:303
  11.5 1.5 %collective-permute-start.3 = (bf16[32,1024]{1,0:T(8,128)(2,1)S(1)}, bf16[32,1024]{1,0:T(8,128)(2,1)S(1)}, u32[]{:S(2)}, u32[]{:S(2)}) collective-permute-start(bf16[32,1024]{1,0:T(8,128)(2,1)S(1)} %get-tuple-element.22), channel_id=1, source_target_pairs={{0,2},{2,0},{4,6},{6,4},{8,10},{10,8},{12,14},{14,12},{16,18},{18,... | collective-permute-start | bytes 196616 | tf_op jit(solution)/shard_map/ppermute | solution.py:272
  13.1 1.5 %collective-permute-start.4 = (bf16[32,1024]{1,0:T(8,128)(2,1)S(1)}, bf16[32,1024]{1,0:T(8,128)(2,1)S(1)}, u32[]{:S(2)}, u32[]{:S(2)}) collective-permute-start(bf16[32,1024]{1,0:T(8,128)(2,1)S(1)} %get-tuple-element.23), channel_id=1, source_target_pairs={{0,6},{2,4},{4,2},{6,0},{8,14},{10,12},{12,10},{14,8},{16,22},{18,... | collective-permute-start | bytes 196616 | tf_op jit(solution)/shard_map/ppermute | solution.py:272
  14.6 0.5 %collective-permute-start.5 = (bf16[32,1024]{1,0:T(8,128)(2,1)S(1)}, bf16[32,1024]{1,0:T(8,128)(2,1)S(1)}, u32[]{:S(2)}, u32[]{:S(2)}) collective-permute-start(bf16[32,1024]{1,0:T(8,128)(2,1)S(1)} %get-tuple-element.24), channel_id=1, source_target_pairs={{0,4},{2,6},{4,0},{6,2},{8,12},{10,14},{12,8},{14,10},{16,20},{18,... | collective-permute-start | bytes 196616 | tf_op jit(solution)/shard_map/ppermute | solution.py:272
  15.1 3.0 %tables.1.refs_4_.refs_1_ = bf16[256,4096]{1,0:T(8,128)(2,1)S(1)} custom-call(s32[16,132]{1,0:T(8,128)S(1)} %get-tuple-element.25.refs_0_, s32[16,132]{1,0:T(8,128)S(1)} %get-tuple-element.26.refs_1_, s32[16,132]{1,0:T(8,128)S(1)} %get-tuple-element.27.refs_2_, s32[16,132]{1,0:T(8,128)S(1)} %get-tuple-element.28.refs_3_, ...), custom_call_target="tpu_custom_call" | custom-call | flops 1254899712 | bytes 8388608 | tf_op jit(solution)/shard_map/tables/pallas_call | solution.py:313
  18.1 0.0 collective-permute-done.3.refs_1_
  18.1 0.2 collective-permute-done.4.refs_2_
  18.2 0.7 %collective-permute-done.5.refs_3_ = bf16[32,1024]{1,0:T(8,128)(2,1)S(1)} collective-permute-done((bf16[32,1024]{1,0:T(8,128)(2,1)S(1)}, bf16[32,1024]{1,0:T(8,128)(2,1)S(1)}, u32[]{:S(2)}, u32[]{:S(2)}) %collective-permute-start.5) | collective-permute-done | bytes 65568 | tf_op jit(solution)/shard_map/ppermute | solution.py:272
  18.9 0.8 %theirs.1 = (bf16[4096,128]{1,0:T(8,128)(2,1)S(1)}, f32[64,256]{1,0:T(8,128)S(1)}) custom-call(bf16[32,1024]{1,0:T(8,128)(2,1)S(1)} %get-tuple-element.21.refs_7_.refs_0_, bf16[32,1024]{1,0:T(8,128)(2,1)S(1)} %collective-permute-done.3.refs_1_, bf16[32,1024]{1,0:T(8,128)(2,1)S(1)} %collective-permute-done.4.refs_2_, ...), custom_call_target="tpu_custom_call" | custom-call | flops 134217728 | bytes 3145728 | tf_op jit(solution)/shard_map/theirs/pallas_call | solution.py:341
  19.8 0.1 collective-permute-start.6
  19.8 0.7 %mine.1 = f32[64,256]{1,0:T(8,128)S(1)} custom-call(bf16[4096,128]{1,0:T(8,128)(2,1)S(1)} %get-tuple-element.33.refs_0_, bf16[256,4096]{1,0:T(8,128)(2,1)S(1)} %tables.1.refs_4_.refs_1_, bf16[256,1024]{1,0:T(8,128)(2,1)S(1)} %get-tuple-element.32.refs_5_.refs_2_), custom_call_target="tpu_custom_call" | custom-call | flops 134217728 | bytes 3145728 | tf_op jit(solution)/shard_map/mine/pallas_call | solution.py:360
  20.5 0.5 %collective-permute-done.6 = f32[64,256]{1,0:T(8,128)S(1)} collective-permute-done((f32[64,256]{1,0:T(8,128)S(1)}, f32[64,256]{1,0:T(8,128)S(1)}, u32[]{:S(2)}, u32[]{:S(2)}) %collective-permute-start.6) | collective-permute-done | bytes 65568 | tf_op jit(solution)/shard_map/ppermute | solution.py:351
  21.1 0.6 %add.3 = f32[64,256]{1,0:T(8,128)} add(f32[64,256]{1,0:T(8,128)S(1)} %mine.1, f32[64,256]{1,0:T(8,128)S(1)} %collective-permute-done.6) | non-fusion elementwise | flops 16384 | bytes 196608 | tf_op jit(solution)/shard_map/add | solution.py:364
Async XLA Ops:
  0.8 7.1 %collective-permute-start.2 = (bf16[80,256]{1,0:T(8,128)(2,1)S(1)}, bf16[80,256]{1,0:T(8,128)(2,1)S(1)}, u32[]{:S(2)}, u32[]{:S(2)}) collective-permute-start(bf16[80,256]{1,0:T(8,128)(2,1)S(1)} %pack.1.refs_7_.refs_0_), channel_id=1, source_target_pairs={{0,24},{2,26},{4,28},{6,30},{8,16},{10,18},{12,20},{14,22},{16,8},... | collective-permute-start | bytes 122888 | tf_op jit(solution)/shard_map/ppermute | solution.py:272
  5.9 4.9 %collective-permute-start.1 = (bf16[80,256]{1,0:T(8,128)(2,1)S(1)}, bf16[80,256]{1,0:T(8,128)(2,1)S(1)}, u32[]{:S(2)}, u32[]{:S(2)}) collective-permute-start(bf16[80,256]{1,0:T(8,128)(2,1)S(1)} %pack.1.refs_7_.refs_0_), channel_id=1, source_target_pairs={{0,16},{2,18},{4,20},{6,22},{8,24},{10,26},{12,28},{14,30},{16,0},... | collective-permute-start | bytes 122888 | tf_op jit(solution)/shard_map/ppermute | solution.py:272
  5.9 4.9 %collective-permute-start = (bf16[80,256]{1,0:T(8,128)(2,1)S(1)}, bf16[80,256]{1,0:T(8,128)(2,1)S(1)}, u32[]{:S(2)}, u32[]{:S(2)}) collective-permute-start(bf16[80,256]{1,0:T(8,128)(2,1)S(1)} %pack.1.refs_7_.refs_0_), channel_id=1, source_target_pairs={{0,8},{2,10},{4,12},{6,14},{8,0},{10,2},{12,4},{14,6},{16,24},{18,... | collective-permute-start | bytes 122888 | tf_op jit(solution)/shard_map/ppermute | solution.py:272
  11.5 6.5 %collective-permute-start.3 = (bf16[32,1024]{1,0:T(8,128)(2,1)S(1)}, bf16[32,1024]{1,0:T(8,128)(2,1)S(1)}, u32[]{:S(2)}, u32[]{:S(2)}) collective-permute-start(bf16[32,1024]{1,0:T(8,128)(2,1)S(1)} %get-tuple-element.22), channel_id=1, source_target_pairs={{0,2},{2,0},{4,6},{6,4},{8,10},{10,8},{12,14},{14,12},{16,18},{18,... | collective-permute-start | bytes 196616 | tf_op jit(solution)/shard_map/ppermute | solution.py:272
  13.1 5.2 %collective-permute-start.4 = (bf16[32,1024]{1,0:T(8,128)(2,1)S(1)}, bf16[32,1024]{1,0:T(8,128)(2,1)S(1)}, u32[]{:S(2)}, u32[]{:S(2)}) collective-permute-start(bf16[32,1024]{1,0:T(8,128)(2,1)S(1)} %get-tuple-element.23), channel_id=1, source_target_pairs={{0,6},{2,4},{4,2},{6,0},{8,14},{10,12},{12,10},{14,8},{16,22},{18,... | collective-permute-start | bytes 196616 | tf_op jit(solution)/shard_map/ppermute | solution.py:272
  14.6 4.4 %collective-permute-start.5 = (bf16[32,1024]{1,0:T(8,128)(2,1)S(1)}, bf16[32,1024]{1,0:T(8,128)(2,1)S(1)}, u32[]{:S(2)}, u32[]{:S(2)}) collective-permute-start(bf16[32,1024]{1,0:T(8,128)(2,1)S(1)} %get-tuple-element.24), channel_id=1, source_target_pairs={{0,4},{2,6},{4,0},{6,2},{8,12},{10,14},{12,8},{14,10},{16,20},{18,... | collective-permute-start | bytes 196616 | tf_op jit(solution)/shard_map/ppermute | solution.py:272
  19.8 1.3 %collective-permute-start.6 = (f32[64,256]{1,0:T(8,128)S(1)}, f32[64,256]{1,0:T(8,128)S(1)}, u32[]{:S(2)}, u32[]{:S(2)}) collective-permute-start(f32[64,256]{1,0:T(8,128)S(1)} %get-tuple-element.34), channel_id=1, source_target_pairs={{0,1},{1,0},{2,3},{3,2},{4,5},{5,4},{6,7},{7,6},{8,9},{9,8},{10,11... | collective-permute-start | bytes 196616 | tf_op jit(solution)/shard_map/ppermute | solution.py:351

commit v6 on v5

--- a/solution.py
+++ b/solution.py
@@ -152,8 +152,9 @@
         right = one(row_of(orbitals) == bpair[:, v : v + 1])
         t_ref[v * beta_blocks : (v + 1) * beta_blocks, :] = dot(left.astype(BF), right).astype(BF)
     high, low = split(dot(t_ref[...], integrals_ref[...]))
-    w_ref[0] = high
-    w_ref[1] = low
+    wide = beta_local * beta_blocks
+    w_ref[:wide] = high
+    w_ref[wide:] = low
     pair = pair_ref[...].astype(F32).T.astype(jnp.int32)
     factor = (1 - 2 * parity_ref[...]).astype(F32)
     slot = slot_ref[...]
@@ -172,18 +173,19 @@
     step = max(1, WIDE // slots)
     for start in range(0, pairs, step):
         hot = hot_ref[start * slots : (start + step) * slots, :]
-        high, low = split(dot_nt(w_ref[0], hot) + dot_nt(w_ref[1], hot))
+        product = dot_nt(w_ref[...], hot)
+        high, low = split(product[:wide] + product[wide:])
         for i in range(step):
             lanes = slice(i * slots, (i + 1) * slots)
             for v in range(beta_local):
-                first = v * 2 * slots
+                columns = slice(v * slots, (v + 1) * slots)
                 for part in range(beta_blocks // beta_local):
-                    row = (part * pairs + start + i) * beta_local
-                    rows = slice(row, row + beta_local)
                     row = v * beta_blocks + part * beta_local
                     source = slice(row, row + beta_local)
-                    out_ref[rows, first : first + slots] = high[source, lanes]
-                    out_ref[rows, first + slots : first + 2 * slots] = low[source, lanes]
+                    row = (2 * part * pairs + start + i) * beta_local
+                    out_ref[row : row + beta_local, columns] = high[source, lanes]
+                    row += pairs * beta_local
+                    out_ref[row : row + beta_local, columns] = low[source, lanes]
 
 
 def right_kernel(strings, width, inner, turn, *refs):
@@ -199,9 +201,7 @@
         x = received[:, tile * both : (tile + 1) * both]
         turned = jnp.concatenate([x[:, group:], x[:, :group]], axis=1)
         for v, (a, b) in ((2 * tile, (x, turned)), (2 * tile + 1, (turned, x))):
-            value = a * low + b * high
-            right_ref[2 * v * slots : (2 * v + 1) * slots, :] = value
-            right_ref[(2 * v + 1) * slots : (2 * v + 2) * slots, :] = value
+            right_ref[v * slots : (v + 1) * slots, :] = a * low + b * high
     sigma_kernel(strings, width, 1, right_ref, table_ref, expand_ref, *rest)
 
 
@@ -210,7 +210,8 @@
     pairs = local_rows // strings // BATCHES
     blocks = columns // width
     rows = pairs * blocks
-    product = dot(table_ref[part * rows : (part + 1) * rows, :], right_ref[...])
+    product = dot(table_ref[part * 2 * rows : (part + 1) * 2 * rows, :], right_ref[...])
+    product = product[:rows] + product[rows:]
     both_parts = jnp.concatenate(split(product), axis=1)
     per_tile = LANES // width
     spread = dot(both_parts, expand_ref[...])
@@ -314,10 +315,10 @@
         lambda *refs: tables_kernel(beta_blocks, outer, inner, *refs),
         in_specs=[pl.BlockSpec(memory_space=pltpu.VMEM)] * len(tables)
         + [pl.BlockSpec(memory_space=pl.ANY)],
-        out_shape=jax.ShapeDtypeStruct((pairs * beta_blocks, 2 * beta_local * slots), BF),
+        out_shape=jax.ShapeDtypeStruct((2 * pairs * beta_blocks, beta_local * slots), BF),
         scratch_shapes=[
             pltpu.VMEM((beta_local * beta_blocks, orbitals), BF),
-            pltpu.VMEM((2, beta_local * beta_blocks, orbitals), BF),
+            pltpu.VMEM((2 * beta_local * beta_blocks, orbitals), BF),
             pltpu.VMEM((pairs * slots, orbitals), BF),
         ],
         compiler_params=pltpu.CompilerParams(vmem_limit_bytes=40 * 2**20),
@@ -340,7 +341,7 @@
     )
     right, theirs = pl.pallas_call(
         lambda *refs: right_kernel(strings, width, inner, turn, *refs),
-        out_shape=[jax.ShapeDtypeStruct((2 * beta_local * slots, both), BF), part],
+        out_shape=[jax.ShapeDtypeStruct((beta_local * slots, both), BF), part],
         name="theirs",
         **call,
     )(*(received[j] for j in turn), table, expand)

time: 22 us -> 21.9 us (level)
  transfers between devices with their start and end apart: 7 -> 7, of which waited for: 5 -> 4; matrix products, arithmetic and copies ran while one was open for 0% -> 0% of each run, Pallas kernels for 22% -> 23%
where the time goes in v6:
time: 21.9 us; the launch traced here: 21.7 us
  starting transfers between devices  9.36 us (43%)
  Pallas kernels  7.38 us (34%)
  waiting for transfers between devices  4.26 us (19%)
  other arithmetic  0.64 us (3%)
    ppermute x6, starting transfers between devices, exchange(): lax.ppermute(x, 'alpha', [(d, d ^ k) for d in range(senders)])  9.3 us
    ppermute x6, waiting for transfers between devices, exchange(): lax.ppermute(x, 'alpha', [(d, d ^ k) for d in range(senders)])  3.72 us
    pallas_call x1, Pallas kernels, on_device(): pl.pallas_call(lambda *refs: tables_kernel(beta_blocks, outer, inner, *re...  3.17 us
    pallas_call x1, Pallas kernels, on_device(): pl.pallas_call(lambda *refs: fetch_kernel(width, *refs), in_specs=[pl.Blo...  1.2 us
    pallas_call x1, Pallas kernels, on_device(): pl.pallas_call(lambda *refs: right_kernel(strings, width, inner, turn, *r...  0.81 us
    pallas_call x1, Pallas kernels, on_device(): pl.pallas_call(pack_kernel, in_specs=[pl.BlockSpec(memory_space=pltpu.HBM...  0.79 us
    pallas_call x1, Pallas kernels, on_device(): pl.pallas_call(lambda *refs: forward_kernel(strings, width, local_rows, s...  0.71 us
    pallas_call x1, Pallas kernels, on_device(): pl.pallas_call(lambda *refs: sigma_kernel(strings, width, 0, *refs), out_...  0.7 us
  transfers between devices with their start and end apart: 7, of which 4 were waited for; matrix products, arithmetic and copies ran while one was open for 0% of the time, Pallas kernels for 23%

profile of v6, /device:TPU:0, one launch (start us, length us, event | category | flops | bytes accessed | tf_op | source)
XLA Modules:
  0.0 21.7 jit_solution(2979547416415194966)
XLA Ops:
  0.0 0.8 %pack.1.refs_7_.refs_0_ = bf16[80,256]{1,0:T(8,128)(2,1)S(1)} custom-call(bf16[64,256]{1,0:T(8,128)(2,1)} %coeffs_ref.1, s32[1,128]{1,0:T(1,128)} %send_ref.1), custom_call_target="tpu_custom_call" | custom-call | tf_op jit(solution)/shard_map/pack/pallas_call | solution.py:278
  0.8 5.1 %collective-permute-start.2 = (bf16[80,256]{1,0:T(8,128)(2,1)S(1)}, bf16[80,256]{1,0:T(8,128)(2,1)S(1)}, u32[]{:S(2)}, u32[]{:S(2)}) collective-permute-start(bf16[80,256]{1,0:T(8,128)(2,1)S(1)} %pack.1.refs_7_.refs_0_), channel_id=1, source_target_pairs={{0,24},{2,26},{4,28},{6,30},{8,16},{10,18},{12,20},{14,22},{16,8},... | collective-permute-start | bytes 122888 | tf_op jit(solution)/shard_map/ppermute | solution.py:273
  5.9 0.0 collective-permute-start.1
  5.9 0.6 %collective-permute-start = (bf16[80,256]{1,0:T(8,128)(2,1)S(1)}, bf16[80,256]{1,0:T(8,128)(2,1)S(1)}, u32[]{:S(2)}, u32[]{:S(2)}) collective-permute-start(bf16[80,256]{1,0:T(8,128)(2,1)S(1)} %pack.1.refs_7_.refs_0_), channel_id=1, source_target_pairs={{0,8},{2,10},{4,12},{6,14},{8,0},{10,2},{12,4},{14,6},{16,24},{18,... | collective-permute-start | bytes 122888 | tf_op jit(solution)/shard_map/ppermute | solution.py:273
  6.6 1.2 %fetch.1 = (s32[16,132]{1,0:T(8,128)S(1)}, s32[16,132]{1,0:T(8,128)S(1)}, s32[16,132]{1,0:T(8,128)S(1)}, s32[16,132]{1,0:T(8,128)S(1)}, s32[16,132]{1,0:T(8,128)...) custom-call(s32[16,132]{1,0:T(8,128)} %refs_0_.1, ...), custom_call_target="tpu_custom_call" | custom-call | tf_op jit(solution)/shard_map/fetch/pallas_call | solution.py:291
  7.8 0.2 collective-permute-done.2.refs_3_
  7.9 2.9 %collective-permute-done.1.refs_2_ = bf16[80,256]{1,0:T(8,128)(2,1)S(1)} collective-permute-done((bf16[80,256]{1,0:T(8,128)(2,1)S(1)}, bf16[80,256]{1,0:T(8,128)(2,1)S(1)}, u32[]{:S(2)}, u32[]{:S(2)}) %collective-permute-start.1) | collective-permute-done | bytes 40992 | tf_op jit(solution)/shard_map/ppermute | solution.py:273
  10.8 0.0 collective-permute-done.refs_1_
  10.8 0.7 %forward.1 = (bf16[32,1024]{1,0:T(8,128)(2,1)S(1)}, bf16[32,1024]{1,0:T(8,128)(2,1)S(1)}, bf16[32,1024]{1,0:T(8,128)(2,1)S(1)}, bf16[32,1024]{1,0:T(8,128)(2,1)S(1)}) custom-call(bf16[80,256]{1,0:T(8,128)(2,1)S(1)} %pack.1.refs_7_.refs_0_, bf16[80,256]{1,0:T(8,128)(2,1)S(1)} %collective-permute-done.refs_1_, ...), custom_call_target="tpu_custom_call" | custom-call | tf_op jit(solution)/shard_map/forward/pallas_call | solution.py:304
  11.5 1.5 %collective-permute-start.3 = (bf16[32,1024]{1,0:T(8,128)(2,1)S(1)}, bf16[32,1024]{1,0:T(8,128)(2,1)S(1)}, u32[]{:S(2)}, u32[]{:S(2)}) collective-permute-start(bf16[32,1024]{1,0:T(8,128)(2,1)S(1)} %get-tuple-element.22), channel_id=1, source_target_pairs={{0,2},{2,0},{4,6},{6,4},{8,10},{10,8},{12,14},{14,12},{16,18},{18,... | collective-permute-start | bytes 196616 | tf_op jit(solution)/shard_map/ppermute | solution.py:273
  13.1 1.5 %collective-permute-start.4 = (bf16[32,1024]{1,0:T(8,128)(2,1)S(1)}, bf16[32,1024]{1,0:T(8,128)(2,1)S(1)}, u32[]{:S(2)}, u32[]{:S(2)}) collective-permute-start(bf16[32,1024]{1,0:T(8,128)(2,1)S(1)} %get-tuple-element.23), channel_id=1, source_target_pairs={{0,6},{2,4},{4,2},{6,0},{8,14},{10,12},{12,10},{14,8},{16,22},{18,... | collective-permute-start | bytes 196616 | tf_op jit(solution)/shard_map/ppermute | solution.py:273
  14.6 0.5 %collective-permute-start.5 = (bf16[32,1024]{1,0:T(8,128)(2,1)S(1)}, bf16[32,1024]{1,0:T(8,128)(2,1)S(1)}, u32[]{:S(2)}, u32[]{:S(2)}) collective-permute-start(bf16[32,1024]{1,0:T(8,128)(2,1)S(1)} %get-tuple-element.24), channel_id=1, source_target_pairs={{0,4},{2,6},{4,0},{6,2},{8,12},{10,14},{12,8},{14,10},{16,20},{18,... | collective-permute-start | bytes 196616 | tf_op jit(solution)/shard_map/ppermute | solution.py:273
  15.1 3.2 %tables.1.refs_4_.refs_1_ = bf16[512,2048]{1,0:T(8,128)(2,1)S(1)} custom-call(s32[16,132]{1,0:T(8,128)S(1)} %get-tuple-element.25.refs_0_, s32[16,132]{1,0:T(8,128)S(1)} %get-tuple-element.26.refs_1_, s32[16,132]{1,0:T(8,128)S(1)} %get-tuple-element.27.refs_2_, s32[16,132]{1,0:T(8,128)S(1)} %get-tuple-element.28.refs_3_, ...), custom_call_target="tpu_custom_call" | custom-call | flops 1254899712 | bytes 8388608 | tf_op jit(solution)/shard_map/tables/pallas_call | solution.py:314
  18.2 0.0 collective-permute-done.3.refs_1_
  18.3 0.0 collective-permute-done.4.refs_2_
  18.3 0.7 %collective-permute-done.5.refs_3_ = bf16[32,1024]{1,0:T(8,128)(2,1)S(1)} collective-permute-done((bf16[32,1024]{1,0:T(8,128)(2,1)S(1)}, bf16[32,1024]{1,0:T(8,128)(2,1)S(1)}, u32[]{:S(2)}, u32[]{:S(2)}) %collective-permute-start.5) | collective-permute-done | bytes 65568 | tf_op jit(solution)/shard_map/ppermute | solution.py:273
  18.9 0.8 %theirs.1 = (bf16[2048,128]{1,0:T(8,128)(2,1)S(1)}, f32[64,256]{1,0:T(8,128)S(1)}) custom-call(bf16[32,1024]{1,0:T(8,128)(2,1)S(1)} %get-tuple-element.21.refs_7_.refs_0_, bf16[32,1024]{1,0:T(8,128)(2,1)S(1)} %collective-permute-done.3.refs_1_, bf16[32,1024]{1,0:T(8,128)(2,1)S(1)} %collective-permute-done.4.refs_2_, ...), custom_call_target="tpu_custom_call" | custom-call | flops 134217728 | bytes 3145728 | tf_op jit(solution)/shard_map/theirs/pallas_call | solution.py:342
  19.7 0.1 collective-permute-start.6
  19.8 0.7 %mine.1 = f32[64,256]{1,0:T(8,128)S(1)} custom-call(bf16[2048,128]{1,0:T(8,128)(2,1)S(1)} %get-tuple-element.33.refs_0_, bf16[512,2048]{1,0:T(8,128)(2,1)S(1)} %tables.1.refs_4_.refs_1_, bf16[256,1024]{1,0:T(8,128)(2,1)S(1)} %get-tuple-element.32.refs_5_.refs_2_), custom_call_target="tpu_custom_call" | custom-call | flops 134217728 | bytes 3145728 | tf_op jit(solution)/shard_map/mine/pallas_call | solution.py:361
  20.5 0.5 %collective-permute-done.6 = f32[64,256]{1,0:T(8,128)S(1)} collective-permute-done((f32[64,256]{1,0:T(8,128)S(1)}, f32[64,256]{1,0:T(8,128)S(1)}, u32[]{:S(2)}, u32[]{:S(2)}) %collective-permute-start.6) | collective-permute-done | bytes 65568 | tf_op jit(solution)/shard_map/ppermute | solution.py:352
  21.1 0.6 %add.3 = f32[64,256]{1,0:T(8,128)} add(f32[64,256]{1,0:T(8,128)S(1)} %mine.1, f32[64,256]{1,0:T(8,128)S(1)} %collective-permute-done.6) | non-fusion elementwise | flops 16384 | bytes 196608 | tf_op jit(solution)/shard_map/add | solution.py:365
Async XLA Ops:
  0.8 7.1 %collective-permute-start.2 = (bf16[80,256]{1,0:T(8,128)(2,1)S(1)}, bf16[80,256]{1,0:T(8,128)(2,1)S(1)}, u32[]{:S(2)}, u32[]{:S(2)}) collective-permute-start(bf16[80,256]{1,0:T(8,128)(2,1)S(1)} %pack.1.refs_7_.refs_0_), channel_id=1, source_target_pairs={{0,24},{2,26},{4,28},{6,30},{8,16},{10,18},{12,20},{14,22},{16,8},... | collective-permute-start | bytes 122888 | tf_op jit(solution)/shard_map/ppermute | solution.py:273
  5.9 4.9 %collective-permute-start.1 = (bf16[80,256]{1,0:T(8,128)(2,1)S(1)}, bf16[80,256]{1,0:T(8,128)(2,1)S(1)}, u32[]{:S(2)}, u32[]{:S(2)}) collective-permute-start(bf16[80,256]{1,0:T(8,128)(2,1)S(1)} %pack.1.refs_7_.refs_0_), channel_id=1, source_target_pairs={{0,16},{2,18},{4,20},{6,22},{8,24},{10,26},{12,28},{14,30},{16,0},... | collective-permute-start | bytes 122888 | tf_op jit(solution)/shard_map/ppermute | solution.py:273
  5.9 4.9 %collective-permute-start = (bf16[80,256]{1,0:T(8,128)(2,1)S(1)}, bf16[80,256]{1,0:T(8,128)(2,1)S(1)}, u32[]{:S(2)}, u32[]{:S(2)}) collective-permute-start(bf16[80,256]{1,0:T(8,128)(2,1)S(1)} %pack.1.refs_7_.refs_0_), channel_id=1, source_target_pairs={{0,8},{2,10},{4,12},{6,14},{8,0},{10,2},{12,4},{14,6},{16,24},{18,... | collective-permute-start | bytes 122888 | tf_op jit(solution)/shard_map/ppermute | solution.py:273
  11.5 6.7 %collective-permute-start.3 = (bf16[32,1024]{1,0:T(8,128)(2,1)S(1)}, bf16[32,1024]{1,0:T(8,128)(2,1)S(1)}, u32[]{:S(2)}, u32[]{:S(2)}) collective-permute-start(bf16[32,1024]{1,0:T(8,128)(2,1)S(1)} %get-tuple-element.22), channel_id=1, source_target_pairs={{0,2},{2,0},{4,6},{6,4},{8,10},{10,8},{12,14},{14,12},{16,18},{18,... | collective-permute-start | bytes 196616 | tf_op jit(solution)/shard_map/ppermute | solution.py:273
  13.1 5.2 %collective-permute-start.4 = (bf16[32,1024]{1,0:T(8,128)(2,1)S(1)}, bf16[32,1024]{1,0:T(8,128)(2,1)S(1)}, u32[]{:S(2)}, u32[]{:S(2)}) collective-permute-start(bf16[32,1024]{1,0:T(8,128)(2,1)S(1)} %get-tuple-element.23), channel_id=1, source_target_pairs={{0,6},{2,4},{4,2},{6,0},{8,14},{10,12},{12,10},{14,8},{16,22},{18,... | collective-permute-start | bytes 196616 | tf_op jit(solution)/shard_map/ppermute | solution.py:273
  14.6 4.4 %collective-permute-start.5 = (bf16[32,1024]{1,0:T(8,128)(2,1)S(1)}, bf16[32,1024]{1,0:T(8,128)(2,1)S(1)}, u32[]{:S(2)}, u32[]{:S(2)}) collective-permute-start(bf16[32,1024]{1,0:T(8,128)(2,1)S(1)} %get-tuple-element.24), channel_id=1, source_target_pairs={{0,4},{2,6},{4,0},{6,2},{8,12},{10,14},{12,8},{14,10},{16,20},{18,... | collective-permute-start | bytes 196616 | tf_op jit(solution)/shard_map/ppermute | solution.py:273
  19.7 1.3 %collective-permute-start.6 = (f32[64,256]{1,0:T(8,128)S(1)}, f32[64,256]{1,0:T(8,128)S(1)}, u32[]{:S(2)}, u32[]{:S(2)}) collective-permute-start(f32[64,256]{1,0:T(8,128)S(1)} %get-tuple-element.34), channel_id=1, source_target_pairs={{0,1},{1,0},{2,3},{3,2},{4,5},{5,4},{6,7},{7,6},{8,9},{9,8},{10,11... | collective-permute-start | bytes 196616 | tf_op jit(solution)/shard_map/ppermute | solution.py:352

commit v7 on v5

--- a/solution.py
+++ b/solution.py
@@ -31,6 +31,12 @@
     if n & (n - 1) == 0:
         return x & (n - 1)
     return lax.rem(x, jnp.int32(n))
+
+
+def turned(x, inner):
+    bits = inner.bit_length() - 1
+    back = sum(((x >> i) & 1) << (bits - 1 - i) for i in range(bits))
+    return jnp.where(lax.axis_index("beta") == 1, back, x)
 
 
 def one(condition):
@@ -105,7 +111,7 @@
     keep = modulo(column_of(outer * rows), strings) == modulo(over(n, width), strings)
     spaced = jnp.where(keep, dot(gathered, spread_ref[...]), 0.0).astype(BF)
     r = column_of(inner * per)
-    receiver = over(r, per) ^ lax.axis_index("alpha")
+    receiver = turned(over(r, per), inner) ^ lax.axis_index("alpha")
     wanted = over(modulo(r, per), CAP) * (slots // BATCHES) + receiver * CAP + modulo(r, CAP)
     wanted = wanted == row_of(slots)
     picks = []
@@ -158,7 +164,7 @@
     factor = (1 - 2 * parity_ref[...]).astype(F32)
     slot = slot_ref[...]
     partner = over(slot, CAP) ^ lax.axis_index("alpha")
-    place = modulo(partner, inner) * outer + over(partner, inner)
+    place = turned(modulo(partner, inner), inner) * outer + over(partner, inner)
     place = place * (BATCHES * CAP) + modulo(slot, CAP)
     for t in range(pairs):
         total = None
@@ -197,8 +203,8 @@
     high = one((batch == 1) & (row_of(both) >= group))
     for tile in range(wide // both):
         x = received[:, tile * both : (tile + 1) * both]
-        turned = jnp.concatenate([x[:, group:], x[:, :group]], axis=1)
-        for v, (a, b) in ((2 * tile, (x, turned)), (2 * tile + 1, (turned, x))):
+        swapped = jnp.concatenate([x[:, group:], x[:, :group]], axis=1)
+        for v, (a, b) in ((2 * tile, (x, swapped)), (2 * tile + 1, (swapped, x))):
             value = a * low + b * high
             right_ref[2 * v * slots : (2 * v + 1) * slots, :] = value
             right_ref[(2 * v + 1) * slots : (2 * v + 2) * slots, :] = value
@@ -306,7 +312,18 @@
         compiler_params=pltpu.CompilerParams(vmem_limit_bytes=40 * 2**20),
         name="forward",
     )(*gathered, spread)
-    received = [exchange(x, j) for j, x in enumerate(outgoing)]
+    bits = inner.bit_length() - 1
+
+    def across(x, j):
+        if not j:
+            return x
+        partners = [int(format(j, "0%db" % bits)[::-1], 2) if c == 1 else j for c in range(cores)]
+        route = [
+            (d * cores + c, (d ^ partners[c]) * cores + c) for d in range(senders) for c in range(cores)
+        ]
+        return lax.ppermute(x, ("alpha", "beta"), route)
+
+    received = [across(x, j) for j, x in enumerate(outgoing)]
     turn = sorted(range(inner), key=lambda j: -format(j or outer * inner * 2 - 1, "b").count("1"))
     turn = turn[:1] + turn[-2:-1] + turn[1:-2] + turn[-1:]
     flops = 2 * beta_local * beta_blocks * orbitals * (orbitals + 2 * pairs * slots)

time: 22 us -> 22 us (level)
    ppermute x0 -> x3, starting transfers between devices: none -> 3.54 us  [across(): return lax.ppermute(x, ('alpha', 'beta'), route)]
    ppermute x6 -> x3, starting transfers between devices: 9.3 us -> 5.76 us  [exchange(): lax.ppermute(x, 'alpha', [(d, d ^ k) for d in range(senders)])]
    ppermute x0 -> x3, waiting for transfers between devices: none -> 0.88 us  [across(): return lax.ppermute(x, ('alpha', 'beta'), route)]
    ppermute x6 -> x3, waiting for transfers between devices: 3.92 us -> 3.05 us  [exchange(): lax.ppermute(x, 'alpha', [(d, d ^ k) for d in range(senders)])]
where the time goes in v7:
time: 22 us; the launch traced here: 21.7 us
  starting transfers between devices  9.37 us (43%)
  Pallas kernels  7.2 us (33%)
  waiting for transfers between devices  4.48 us (20%)
  other arithmetic  0.64 us (3%)
    ppermute x3, starting transfers between devices, exchange(): lax.ppermute(x, 'alpha', [(d, d ^ k) for d in range(senders)])  5.76 us
    ppermute x3, starting transfers between devices, across(): return lax.ppermute(x, ('alpha', 'beta'), route)  3.54 us
    ppermute x3, waiting for transfers between devices, exchange(): lax.ppermute(x, 'alpha', [(d, d ^ k) for d in range(senders)])  3.05 us
    pallas_call x1, Pallas kernels, on_device(): pl.pallas_call(lambda *refs: tables_kernel(beta_blocks, outer, inner, *re...  2.97 us
    pallas_call x1, Pallas kernels, on_device(): pl.pallas_call(lambda *refs: fetch_kernel(width, *refs), in_specs=[pl.Blo...  1.2 us
    ppermute x3, waiting for transfers between devices, across(): return lax.ppermute(x, ('alpha', 'beta'), route)  0.88 us
    pallas_call x1, Pallas kernels, on_device(): pl.pallas_call(lambda *refs: right_kernel(strings, width, inner, turn, *r...  0.84 us
    pallas_call x1, Pallas kernels, on_device(): pl.pallas_call(pack_kernel, in_specs=[pl.BlockSpec(memory_space=pltpu.HBM...  0.79 us
  transfers between devices with their start and end apart: 7, of which 5 were waited for; matrix products, arithmetic and copies ran while one was open for 0% of the time, Pallas kernels for 22%

profile of v7, /device:TPU:0, one launch (start us, length us, event | category | flops | bytes accessed | tf_op | source)
XLA Modules:
  0.0 21.7 jit_solution(7652797476787755379)
XLA Ops:
  0.0 0.8 %pack.1.refs_7_.refs_0_ = bf16[80,256]{1,0:T(8,128)(2,1)S(1)} custom-call(bf16[64,256]{1,0:T(8,128)(2,1)} %coeffs_ref.1, s32[1,128]{1,0:T(1,128)} %send_ref.1), custom_call_target="tpu_custom_call" | custom-call | tf_op jit(solution)/shard_map/pack/pallas_call | solution.py:283
  0.8 5.1 %collective-permute-start.2 = (bf16[80,256]{1,0:T(8,128)(2,1)S(1)}, bf16[80,256]{1,0:T(8,128)(2,1)S(1)}, u32[]{:S(2)}, u32[]{:S(2)}) collective-permute-start(bf16[80,256]{1,0:T(8,128)(2,1)S(1)} %pack.1.refs_7_.refs_0_), channel_id=1, source_target_pairs={{0,24},{2,26},{4,28},{6,30},{8,16},{10,18},{12,20},{14,22},{16,8},... | collective-permute-start | bytes 122888 | tf_op jit(solution)/shard_map/ppermute | solution.py:278
  5.9 0.0 collective-permute-start.1
  5.9 0.6 %collective-permute-start = (bf16[80,256]{1,0:T(8,128)(2,1)S(1)}, bf16[80,256]{1,0:T(8,128)(2,1)S(1)}, u32[]{:S(2)}, u32[]{:S(2)}) collective-permute-start(bf16[80,256]{1,0:T(8,128)(2,1)S(1)} %pack.1.refs_7_.refs_0_), channel_id=1, source_target_pairs={{0,8},{2,10},{4,12},{6,14},{8,0},{10,2},{12,4},{14,6},{16,24},{18,... | collective-permute-start | bytes 122888 | tf_op jit(solution)/shard_map/ppermute | solution.py:278
  6.6 1.2 %fetch.1 = (s32[16,132]{1,0:T(8,128)S(1)}, s32[16,132]{1,0:T(8,128)S(1)}, s32[16,132]{1,0:T(8,128)S(1)}, s32[16,132]{1,0:T(8,128)S(1)}, s32[16,132]{1,0:T(8,128)...) custom-call(s32[16,132]{1,0:T(8,128)} %refs_0_.1, ...), custom_call_target="tpu_custom_call" | custom-call | tf_op jit(solution)/shard_map/fetch/pallas_call | solution.py:296
  7.8 0.2 collective-permute-done.2.refs_3_
  7.9 2.9 %collective-permute-done.1.refs_2_ = bf16[80,256]{1,0:T(8,128)(2,1)S(1)} collective-permute-done((bf16[80,256]{1,0:T(8,128)(2,1)S(1)}, bf16[80,256]{1,0:T(8,128)(2,1)S(1)}, u32[]{:S(2)}, u32[]{:S(2)}) %collective-permute-start.1) | collective-permute-done | bytes 40992 | tf_op jit(solution)/shard_map/ppermute | solution.py:278
  10.8 0.0 collective-permute-done.refs_1_
  10.8 0.7 %forward.1 = (bf16[32,1024]{1,0:T(8,128)(2,1)S(1)}, bf16[32,1024]{1,0:T(8,128)(2,1)S(1)}, bf16[32,1024]{1,0:T(8,128)(2,1)S(1)}, bf16[32,1024]{1,0:T(8,128)(2,1)S(1)}) custom-call(bf16[80,256]{1,0:T(8,128)(2,1)S(1)} %pack.1.refs_7_.refs_0_, bf16[80,256]{1,0:T(8,128)(2,1)S(1)} %collective-permute-done.refs_1_, ...), custom_call_target="tpu_custom_call" | custom-call | tf_op jit(solution)/shard_map/forward/pallas_call | solution.py:309
  11.5 1.5 %collective-permute-start.3 = (bf16[32,1024]{1,0:T(8,128)(2,1)S(1)}, bf16[32,1024]{1,0:T(8,128)(2,1)S(1)}, u32[]{:S(2)}, u32[]{:S(2)}) collective-permute-start(bf16[32,1024]{1,0:T(8,128)(2,1)S(1)} %get-tuple-element.22), channel_id=1, source_target_pairs={{0,2},{1,5},{2,0},{3,7},{4,6},{5,1},{6,4},{7,3},{8,10},{9,13},{10,... | collective-permute-start | bytes 196616 | tf_op jit(solution)/shard_map/ppermute | solution.py:324
  13.1 1.5 %collective-permute-start.4 = (bf16[32,1024]{1,0:T(8,128)(2,1)S(1)}, bf16[32,1024]{1,0:T(8,128)(2,1)S(1)}, u32[]{:S(2)}, u32[]{:S(2)}) collective-permute-start(bf16[32,1024]{1,0:T(8,128)(2,1)S(1)} %get-tuple-element.23), channel_id=1, source_target_pairs={{0,6},{1,7},{2,4},{3,5},{4,2},{5,3},{6,0},{7,1},{8,14},{9,15},{10,... | collective-permute-start | bytes 196616 | tf_op jit(solution)/shard_map/ppermute | solution.py:324
  14.6 0.5 %collective-permute-start.5 = (bf16[32,1024]{1,0:T(8,128)(2,1)S(1)}, bf16[32,1024]{1,0:T(8,128)(2,1)S(1)}, u32[]{:S(2)}, u32[]{:S(2)}) collective-permute-start(bf16[32,1024]{1,0:T(8,128)(2,1)S(1)} %get-tuple-element.24), channel_id=1, source_target_pairs={{0,4},{1,3},{2,6},{3,1},{4,0},{5,7},{6,2},{7,5},{8,12},{9,11},{10,... | collective-permute-start | bytes 196616 | tf_op jit(solution)/shard_map/ppermute | solution.py:324
  15.1 3.0 %tables.1.refs_4_.refs_1_ = bf16[256,4096]{1,0:T(8,128)(2,1)S(1)} custom-call(s32[16,132]{1,0:T(8,128)S(1)} %get-tuple-element.25.refs_0_, s32[16,132]{1,0:T(8,128)S(1)} %get-tuple-element.26.refs_1_, s32[16,132]{1,0:T(8,128)S(1)} %get-tuple-element.27.refs_2_, s32[16,132]{1,0:T(8,128)S(1)} %get-tuple-element.28.refs_3_, ...), custom_call_target="tpu_custom_call" | custom-call | flops 1254899712 | bytes 8388608 | tf_op jit(solution)/shard_map/tables/pallas_call | solution.py:330
  18.0 0.0 collective-permute-done.3.refs_1_
  18.1 0.2 collective-permute-done.4.refs_2_
  18.2 0.7 %collective-permute-done.5.refs_3_ = bf16[32,1024]{1,0:T(8,128)(2,1)S(1)} collective-permute-done((bf16[32,1024]{1,0:T(8,128)(2,1)S(1)}, bf16[32,1024]{1,0:T(8,128)(2,1)S(1)}, u32[]{:S(2)}, u32[]{:S(2)}) %collective-permute-start.5) | collective-permute-done | bytes 65568 | tf_op jit(solution)/shard_map/ppermute | solution.py:324
  18.9 0.8 %theirs.1 = (bf16[4096,128]{1,0:T(8,128)(2,1)S(1)}, f32[64,256]{1,0:T(8,128)S(1)}) custom-call(bf16[32,1024]{1,0:T(8,128)(2,1)S(1)} %get-tuple-element.21.refs_7_.refs_0_, bf16[32,1024]{1,0:T(8,128)(2,1)S(1)} %collective-permute-done.3.refs_1_, bf16[32,1024]{1,0:T(8,128)(2,1)S(1)} %collective-permute-done.4.refs_2_, ...), custom_call_target="tpu_custom_call" | custom-call | flops 134217728 | bytes 3145728 | tf_op jit(solution)/shard_map/theirs/pallas_call | solution.py:358
  19.8 0.1 collective-permute-start.6
  19.8 0.7 %mine.1 = f32[64,256]{1,0:T(8,128)S(1)} custom-call(bf16[4096,128]{1,0:T(8,128)(2,1)S(1)} %get-tuple-element.33.refs_0_, bf16[256,4096]{1,0:T(8,128)(2,1)S(1)} %tables.1.refs_4_.refs_1_, bf16[256,1024]{1,0:T(8,128)(2,1)S(1)} %get-tuple-element.32.refs_5_.refs_2_), custom_call_target="tpu_custom_call" | custom-call | flops 134217728 | bytes 3145728 | tf_op jit(solution)/shard_map/mine/pallas_call | solution.py:377
  20.5 0.5 %collective-permute-done.6 = f32[64,256]{1,0:T(8,128)S(1)} collective-permute-done((f32[64,256]{1,0:T(8,128)S(1)}, f32[64,256]{1,0:T(8,128)S(1)}, u32[]{:S(2)}, u32[]{:S(2)}) %collective-permute-start.6) | collective-permute-done | bytes 65568 | tf_op jit(solution)/shard_map/ppermute | solution.py:368
  21.1 0.6 %add.3 = f32[64,256]{1,0:T(8,128)} add(f32[64,256]{1,0:T(8,128)S(1)} %mine.1, f32[64,256]{1,0:T(8,128)S(1)} %collective-permute-done.6) | non-fusion elementwise | flops 16384 | bytes 196608 | tf_op jit(solution)/shard_map/add | solution.py:381
Async XLA Ops:
  0.8 7.1 %collective-permute-start.2 = (bf16[80,256]{1,0:T(8,128)(2,1)S(1)}, bf16[80,256]{1,0:T(8,128)(2,1)S(1)}, u32[]{:S(2)}, u32[]{:S(2)}) collective-permute-start(bf16[80,256]{1,0:T(8,128)(2,1)S(1)} %pack.1.refs_7_.refs_0_), channel_id=1, source_target_pairs={{0,24},{2,26},{4,28},{6,30},{8,16},{10,18},{12,20},{14,22},{16,8},... | collective-permute-start | bytes 122888 | tf_op jit(solution)/shard_map/ppermute | solution.py:278
  5.9 4.9 %collective-permute-start.1 = (bf16[80,256]{1,0:T(8,128)(2,1)S(1)}, bf16[80,256]{1,0:T(8,128)(2,1)S(1)}, u32[]{:S(2)}, u32[]{:S(2)}) collective-permute-start(bf16[80,256]{1,0:T(8,128)(2,1)S(1)} %pack.1.refs_7_.refs_0_), channel_id=1, source_target_pairs={{0,16},{2,18},{4,20},{6,22},{8,24},{10,26},{12,28},{14,30},{16,0},... | collective-permute-start | bytes 122888 | tf_op jit(solution)/shard_map/ppermute | solution.py:278
  5.9 4.9 %collective-permute-start = (bf16[80,256]{1,0:T(8,128)(2,1)S(1)}, bf16[80,256]{1,0:T(8,128)(2,1)S(1)}, u32[]{:S(2)}, u32[]{:S(2)}) collective-permute-start(bf16[80,256]{1,0:T(8,128)(2,1)S(1)} %pack.1.refs_7_.refs_0_), channel_id=1, source_target_pairs={{0,8},{2,10},{4,12},{6,14},{8,0},{10,2},{12,4},{14,6},{16,24},{18,... | collective-permute-start | bytes 122888 | tf_op jit(solution)/shard_map/ppermute | solution.py:278
  11.5 6.5 %collective-permute-start.3 = (bf16[32,1024]{1,0:T(8,128)(2,1)S(1)}, bf16[32,1024]{1,0:T(8,128)(2,1)S(1)}, u32[]{:S(2)}, u32[]{:S(2)}) collective-permute-start(bf16[32,1024]{1,0:T(8,128)(2,1)S(1)} %get-tuple-element.22), channel_id=1, source_target_pairs={{0,2},{1,5},{2,0},{3,7},{4,6},{5,1},{6,4},{7,3},{8,10},{9,13},{10,... | collective-permute-start | bytes 196616 | tf_op jit(solution)/shard_map/ppermute | solution.py:324
  13.1 5.2 %collective-permute-start.4 = (bf16[32,1024]{1,0:T(8,128)(2,1)S(1)}, bf16[32,1024]{1,0:T(8,128)(2,1)S(1)}, u32[]{:S(2)}, u32[]{:S(2)}) collective-permute-start(bf16[32,1024]{1,0:T(8,128)(2,1)S(1)} %get-tuple-element.23), channel_id=1, source_target_pairs={{0,6},{1,7},{2,4},{3,5},{4,2},{5,3},{6,0},{7,1},{8,14},{9,15},{10,... | collective-permute-start | bytes 196616 | tf_op jit(solution)/shard_map/ppermute | solution.py:324
  14.6 4.4 %collective-permute-start.5 = (bf16[32,1024]{1,0:T(8,128)(2,1)S(1)}, bf16[32,1024]{1,0:T(8,128)(2,1)S(1)}, u32[]{:S(2)}, u32[]{:S(2)}) collective-permute-start(bf16[32,1024]{1,0:T(8,128)(2,1)S(1)} %get-tuple-element.24), channel_id=1, source_target_pairs={{0,4},{1,3},{2,6},{3,1},{4,0},{5,7},{6,2},{7,5},{8,12},{9,11},{10,... | collective-permute-start | bytes 196616 | tf_op jit(solution)/shard_map/ppermute | solution.py:324
  19.8 1.3 %collective-permute-start.6 = (f32[64,256]{1,0:T(8,128)S(1)}, f32[64,256]{1,0:T(8,128)S(1)}, u32[]{:S(2)}, u32[]{:S(2)}) collective-permute-start(f32[64,256]{1,0:T(8,128)S(1)} %get-tuple-element.34), channel_id=1, source_target_pairs={{0,1},{1,0},{2,3},{3,2},{4,5},{5,4},{6,7},{7,6},{8,9},{9,8},{10,11... | collective-permute-start | bytes 196616 | tf_op jit(solution)/shard_map/ppermute | solution.py:368

commit v8 on v7

--- a/solution.py
+++ b/solution.py
@@ -325,7 +325,6 @@
 
     received = [across(x, j) for j, x in enumerate(outgoing)]
     turn = sorted(range(inner), key=lambda j: -format(j or outer * inner * 2 - 1, "b").count("1"))
-    turn = turn[:1] + turn[-2:-1] + turn[1:-2] + turn[-1:]
     flops = 2 * beta_local * beta_blocks * orbitals * (orbitals + 2 * pairs * slots)
     table = pl.pallas_call(
         lambda *refs: tables_kernel(beta_blocks, outer, inner, *refs),

time: 22 us -> 21.9 us (level)
  transfers between devices with their start and end apart: 7 -> 7, of which waited for: 5 -> 5; matrix products, arithmetic and copies ran while one was open for 0% -> 0% of each run, Pallas kernels for 22% -> 23%
where the time goes in v8:
time: 21.9 us; the launch traced here: 21.6 us
  starting transfers between devices  9.37 us (43%)
  Pallas kernels  7.21 us (33%)
  waiting for transfers between devices  4.35 us (20%)
  other arithmetic  0.64 us (3%)
    ppermute x3, starting transfers between devices, exchange(): lax.ppermute(x, 'alpha', [(d, d ^ k) for d in range(senders)])  5.76 us
    ppermute x3, starting transfers between devices, across(): return lax.ppermute(x, ('alpha', 'beta'), route)  3.54 us
    ppermute x3, waiting for transfers between devices, exchange(): lax.ppermute(x, 'alpha', [(d, d ^ k) for d in range(senders)])  3.05 us
    pallas_call x1, Pallas kernels, on_device(): pl.pallas_call(lambda *refs: tables_kernel(beta_blocks, outer, inner, *re...  2.98 us
    pallas_call x1, Pallas kernels, on_device(): pl.pallas_call(lambda *refs: fetch_kernel(width, *refs), in_specs=[pl.Blo...  1.2 us
    pallas_call x1, Pallas kernels, on_device(): pl.pallas_call(lambda *refs: right_kernel(strings, width, inner, turn, *r...  0.84 us
    pallas_call x1, Pallas kernels, on_device(): pl.pallas_call(pack_kernel, in_specs=[pl.BlockSpec(memory_space=pltpu.HBM...  0.79 us
    ppermute x3, waiting for transfers between devices, across(): return lax.ppermute(x, ('alpha', 'beta'), route)  0.76 us
  transfers between devices with their start and end apart: 7, of which 5 were waited for; matrix products, arithmetic and copies ran while one was open for 0% of the time, Pallas kernels for 23%

profile of v8, /device:TPU:0, one launch (start us, length us, event | category | flops | bytes accessed | tf_op | source)
XLA Modules:
  0.0 21.6 jit_solution(1345287137777242657)
XLA Ops:
  0.0 0.8 %pack.1.refs_7_.refs_0_ = bf16[80,256]{1,0:T(8,128)(2,1)S(1)} custom-call(bf16[64,256]{1,0:T(8,128)(2,1)} %coeffs_ref.1, s32[1,128]{1,0:T(1,128)} %send_ref.1), custom_call_target="tpu_custom_call" | custom-call | tf_op jit(solution)/shard_map/pack/pallas_call | solution.py:283
  0.8 5.1 %collective-permute-start.2 = (bf16[80,256]{1,0:T(8,128)(2,1)S(1)}, bf16[80,256]{1,0:T(8,128)(2,1)S(1)}, u32[]{:S(2)}, u32[]{:S(2)}) collective-permute-start(bf16[80,256]{1,0:T(8,128)(2,1)S(1)} %pack.1.refs_7_.refs_0_), channel_id=1, source_target_pairs={{0,24},{2,26},{4,28},{6,30},{8,16},{10,18},{12,20},{14,22},{16,8},... | collective-permute-start | bytes 122888 | tf_op jit(solution)/shard_map/ppermute | solution.py:278
  5.9 0.0 collective-permute-start.1
  5.9 0.6 %collective-permute-start = (bf16[80,256]{1,0:T(8,128)(2,1)S(1)}, bf16[80,256]{1,0:T(8,128)(2,1)S(1)}, u32[]{:S(2)}, u32[]{:S(2)}) collective-permute-start(bf16[80,256]{1,0:T(8,128)(2,1)S(1)} %pack.1.refs_7_.refs_0_), channel_id=1, source_target_pairs={{0,8},{2,10},{4,12},{6,14},{8,0},{10,2},{12,4},{14,6},{16,24},{18,... | collective-permute-start | bytes 122888 | tf_op jit(solution)/shard_map/ppermute | solution.py:278
  6.6 1.2 %fetch.1 = (s32[16,132]{1,0:T(8,128)S(1)}, s32[16,132]{1,0:T(8,128)S(1)}, s32[16,132]{1,0:T(8,128)S(1)}, s32[16,132]{1,0:T(8,128)S(1)}, s32[16,132]{1,0:T(8,128)...) custom-call(s32[16,132]{1,0:T(8,128)} %refs_0_.1, ...), custom_call_target="tpu_custom_call" | custom-call | tf_op jit(solution)/shard_map/fetch/pallas_call | solution.py:296
  7.8 0.2 collective-permute-done.2.refs_3_
  7.9 2.9 %collective-permute-done.1.refs_2_ = bf16[80,256]{1,0:T(8,128)(2,1)S(1)} collective-permute-done((bf16[80,256]{1,0:T(8,128)(2,1)S(1)}, bf16[80,256]{1,0:T(8,128)(2,1)S(1)}, u32[]{:S(2)}, u32[]{:S(2)}) %collective-permute-start.1) | collective-permute-done | bytes 40992 | tf_op jit(solution)/shard_map/ppermute | solution.py:278
  10.8 0.0 collective-permute-done.refs_1_
  10.8 0.7 %forward.1 = (bf16[32,1024]{1,0:T(8,128)(2,1)S(1)}, bf16[32,1024]{1,0:T(8,128)(2,1)S(1)}, bf16[32,1024]{1,0:T(8,128)(2,1)S(1)}, bf16[32,1024]{1,0:T(8,128)(2,1)S(1)}) custom-call(bf16[80,256]{1,0:T(8,128)(2,1)S(1)} %pack.1.refs_7_.refs_0_, bf16[80,256]{1,0:T(8,128)(2,1)S(1)} %collective-permute-done.refs_1_, ...), custom_call_target="tpu_custom_call" | custom-call | tf_op jit(solution)/shard_map/forward/pallas_call | solution.py:309
  11.5 2.5 %collective-permute-start.3 = (bf16[32,1024]{1,0:T(8,128)(2,1)S(1)}, bf16[32,1024]{1,0:T(8,128)(2,1)S(1)}, u32[]{:S(2)}, u32[]{:S(2)}) collective-permute-start(bf16[32,1024]{1,0:T(8,128)(2,1)S(1)} %get-tuple-element.22), channel_id=1, source_target_pairs={{0,6},{1,7},{2,4},{3,5},{4,2},{5,3},{6,0},{7,1},{8,14},{9,15},{10,... | collective-permute-start | bytes 196616 | tf_op jit(solution)/shard_map/ppermute | solution.py:324
  14.0 0.5 %collective-permute-start.4 = (bf16[32,1024]{1,0:T(8,128)(2,1)S(1)}, bf16[32,1024]{1,0:T(8,128)(2,1)S(1)}, u32[]{:S(2)}, u32[]{:S(2)}) collective-permute-start(bf16[32,1024]{1,0:T(8,128)(2,1)S(1)} %get-tuple-element.23), channel_id=1, source_target_pairs={{0,2},{1,5},{2,0},{3,7},{4,6},{5,1},{6,4},{7,3},{8,10},{9,13},{10,... | collective-permute-start | bytes 196616 | tf_op jit(solution)/shard_map/ppermute | solution.py:324
  14.6 0.5 %collective-permute-start.5 = (bf16[32,1024]{1,0:T(8,128)(2,1)S(1)}, bf16[32,1024]{1,0:T(8,128)(2,1)S(1)}, u32[]{:S(2)}, u32[]{:S(2)}) collective-permute-start(bf16[32,1024]{1,0:T(8,128)(2,1)S(1)} %get-tuple-element.24), channel_id=1, source_target_pairs={{0,4},{1,3},{2,6},{3,1},{4,0},{5,7},{6,2},{7,5},{8,12},{9,11},{10,... | collective-permute-start | bytes 196616 | tf_op jit(solution)/shard_map/ppermute | solution.py:324
  15.1 3.0 %tables.1.refs_4_.refs_1_ = bf16[256,4096]{1,0:T(8,128)(2,1)S(1)} custom-call(s32[16,132]{1,0:T(8,128)S(1)} %get-tuple-element.25.refs_0_, s32[16,132]{1,0:T(8,128)S(1)} %get-tuple-element.26.refs_1_, s32[16,132]{1,0:T(8,128)S(1)} %get-tuple-element.27.refs_2_, s32[16,132]{1,0:T(8,128)S(1)} %get-tuple-element.28.refs_3_, ...), custom_call_target="tpu_custom_call" | custom-call | flops 1254899712 | bytes 8388608 | tf_op jit(solution)/shard_map/tables/pallas_call | solution.py:329
  18.1 0.0 collective-permute-done.3.refs_1_
  18.1 0.2 %collective-permute-done.4.refs_2_ = bf16[32,1024]{1,0:T(8,128)(2,1)S(1)} collective-permute-done((bf16[32,1024]{1,0:T(8,128)(2,1)S(1)}, bf16[32,1024]{1,0:T(8,128)(2,1)S(1)}, u32[]{:S(2)}, u32[]{:S(2)}) %collective-permute-start.4) | collective-permute-done | bytes 65568 | tf_op jit(solution)/shard_map/ppermute | solution.py:324
  18.3 0.5 %collective-permute-done.5.refs_3_ = bf16[32,1024]{1,0:T(8,128)(2,1)S(1)} collective-permute-done((bf16[32,1024]{1,0:T(8,128)(2,1)S(1)}, bf16[32,1024]{1,0:T(8,128)(2,1)S(1)}, u32[]{:S(2)}, u32[]{:S(2)}) %collective-permute-start.5) | collective-permute-done | bytes 65568 | tf_op jit(solution)/shard_map/ppermute | solution.py:324
  18.8 0.8 %theirs.1 = (bf16[4096,128]{1,0:T(8,128)(2,1)S(1)}, f32[64,256]{1,0:T(8,128)S(1)}) custom-call(bf16[32,1024]{1,0:T(8,128)(2,1)S(1)} %get-tuple-element.21.refs_7_.refs_0_, bf16[32,1024]{1,0:T(8,128)(2,1)S(1)} %collective-permute-done.3.refs_1_, bf16[32,1024]{1,0:T(8,128)(2,1)S(1)} %collective-permute-done.4.refs_2_, ...), custom_call_target="tpu_custom_call" | custom-call | flops 134217728 | bytes 3145728 | tf_op jit(solution)/shard_map/theirs/pallas_call | solution.py:357
  19.7 0.1 collective-permute-start.6
  19.7 0.7 %mine.1 = f32[64,256]{1,0:T(8,128)S(1)} custom-call(bf16[4096,128]{1,0:T(8,128)(2,1)S(1)} %get-tuple-element.33.refs_0_, bf16[256,4096]{1,0:T(8,128)(2,1)S(1)} %tables.1.refs_4_.refs_1_, bf16[256,1024]{1,0:T(8,128)(2,1)S(1)} %get-tuple-element.32.refs_5_.refs_2_), custom_call_target="tpu_custom_call" | custom-call | flops 134217728 | bytes 3145728 | tf_op jit(solution)/shard_map/mine/pallas_call | solution.py:376
  20.4 0.5 %collective-permute-done.6 = f32[64,256]{1,0:T(8,128)S(1)} collective-permute-done((f32[64,256]{1,0:T(8,128)S(1)}, f32[64,256]{1,0:T(8,128)S(1)}, u32[]{:S(2)}, u32[]{:S(2)}) %collective-permute-start.6) | collective-permute-done | bytes 65568 | tf_op jit(solution)/shard_map/ppermute | solution.py:367
  21.0 0.6 %add.3 = f32[64,256]{1,0:T(8,128)} add(f32[64,256]{1,0:T(8,128)S(1)} %mine.1, f32[64,256]{1,0:T(8,128)S(1)} %collective-permute-done.6) | non-fusion elementwise | flops 16384 | bytes 196608 | tf_op jit(solution)/shard_map/add | solution.py:380
Async XLA Ops:
  0.8 7.1 %collective-permute-start.2 = (bf16[80,256]{1,0:T(8,128)(2,1)S(1)}, bf16[80,256]{1,0:T(8,128)(2,1)S(1)}, u32[]{:S(2)}, u32[]{:S(2)}) collective-permute-start(bf16[80,256]{1,0:T(8,128)(2,1)S(1)} %pack.1.refs_7_.refs_0_), channel_id=1, source_target_pairs={{0,24},{2,26},{4,28},{6,30},{8,16},{10,18},{12,20},{14,22},{16,8},... | collective-permute-start | bytes 122888 | tf_op jit(solution)/shard_map/ppermute | solution.py:278
  5.9 4.9 %collective-permute-start.1 = (bf16[80,256]{1,0:T(8,128)(2,1)S(1)}, bf16[80,256]{1,0:T(8,128)(2,1)S(1)}, u32[]{:S(2)}, u32[]{:S(2)}) collective-permute-start(bf16[80,256]{1,0:T(8,128)(2,1)S(1)} %pack.1.refs_7_.refs_0_), channel_id=1, source_target_pairs={{0,16},{2,18},{4,20},{6,22},{8,24},{10,26},{12,28},{14,30},{16,0},... | collective-permute-start | bytes 122888 | tf_op jit(solution)/shard_map/ppermute | solution.py:278
  5.9 4.9 %collective-permute-start = (bf16[80,256]{1,0:T(8,128)(2,1)S(1)}, bf16[80,256]{1,0:T(8,128)(2,1)S(1)}, u32[]{:S(2)}, u32[]{:S(2)}) collective-permute-start(bf16[80,256]{1,0:T(8,128)(2,1)S(1)} %pack.1.refs_7_.refs_0_), channel_id=1, source_target_pairs={{0,8},{2,10},{4,12},{6,14},{8,0},{10,2},{12,4},{14,6},{16,24},{18,... | collective-permute-start | bytes 122888 | tf_op jit(solution)/shard_map/ppermute | solution.py:278
  11.5 6.5 %collective-permute-start.3 = (bf16[32,1024]{1,0:T(8,128)(2,1)S(1)}, bf16[32,1024]{1,0:T(8,128)(2,1)S(1)}, u32[]{:S(2)}, u32[]{:S(2)}) collective-permute-start(bf16[32,1024]{1,0:T(8,128)(2,1)S(1)} %get-tuple-element.22), channel_id=1, source_target_pairs={{0,6},{1,7},{2,4},{3,5},{4,2},{5,3},{6,0},{7,1},{8,14},{9,15},{10,... | collective-permute-start | bytes 196616 | tf_op jit(solution)/shard_map/ppermute | solution.py:324
  14.0 4.3 %collective-permute-start.4 = (bf16[32,1024]{1,0:T(8,128)(2,1)S(1)}, bf16[32,1024]{1,0:T(8,128)(2,1)S(1)}, u32[]{:S(2)}, u32[]{:S(2)}) collective-permute-start(bf16[32,1024]{1,0:T(8,128)(2,1)S(1)} %get-tuple-element.23), channel_id=1, source_target_pairs={{0,2},{1,5},{2,0},{3,7},{4,6},{5,1},{6,4},{7,3},{8,10},{9,13},{10,... | collective-permute-start | bytes 196616 | tf_op jit(solution)/shard_map/ppermute | solution.py:324
  14.6 4.3 %collective-permute-start.5 = (bf16[32,1024]{1,0:T(8,128)(2,1)S(1)}, bf16[32,1024]{1,0:T(8,128)(2,1)S(1)}, u32[]{:S(2)}, u32[]{:S(2)}) collective-permute-start(bf16[32,1024]{1,0:T(8,128)(2,1)S(1)} %get-tuple-element.24), channel_id=1, source_target_pairs={{0,4},{1,3},{2,6},{3,1},{4,0},{5,7},{6,2},{7,5},{8,12},{9,11},{10,... | collective-permute-start | bytes 196616 | tf_op jit(solution)/shard_map/ppermute | solution.py:324
  19.7 1.3 %collective-permute-start.6 = (f32[64,256]{1,0:T(8,128)S(1)}, f32[64,256]{1,0:T(8,128)S(1)}, u32[]{:S(2)}, u32[]{:S(2)}) collective-permute-start(f32[64,256]{1,0:T(8,128)S(1)} %get-tuple-element.34), channel_id=1, source_target_pairs={{0,1},{1,0},{2,3},{3,2},{4,5},{5,4},{6,7},{7,6},{8,9},{9,8},{10,11... | collective-permute-start | bytes 196616 | tf_op jit(solution)/shard_map/ppermute | solution.py:367
